TPU v7x, 256 devices: a whole 4x4x8 slice. The times are simulated.
256 devices in a mesh: leaf: 64 (over x, z, core), probe: 4 (over y).
Axes of the slice: x: 4, y: 4, z: 8, core: 2. Of those that a mesh axis runs over, the one named last changes fastest.
Arguments:
- probes: float32 [64, 131072], P('probe', 'leaf'), parts along dimension 0, may hold values from -6 to 6
- perm: int32 [131072], P('leaf'), may hold values from 0 to 131071, as said below
- points: float32 [3, 131072], P(None, 'leaf'), may hold values from -4.2 to 4.2
- anchors: float32 [3, 32768], P(None, 'leaf'), may hold values from -4.2 to 4.2
- trans_low: bfloat16 [64, 6, 128, 128], P('leaf'), may hold values from -0.375 to 0.375
- couple_low: bfloat16 [64, 3, 128, 128], P('leaf'), may hold values from -0.25 to 0.25
- trans_top: bfloat16 [126, 128, 128], replicated, may hold values from -0.375 to 0.375
- couple_top: bfloat16 [63, 128, 128], replicated, may hold values from -0.25 to 0.25
Outputs:
- kernel_times: float32 [64, 131072], P('probe', 'leaf'), parts along dimension 0
There are 4 independent parts, one for each index of `probe`. A program takes and returns all parts, laid end to end along the dimension named above; an argument that names none is the same for every part. Nothing has to cross between parts.
Inputs may be any that keep to these rules, and one draw needn't show every extreme that they name: perm is a permutation of the 131072 points; the 2048 positions of each device take exactly 32 points from the 2048 initial points of every device.
All inputs are finite; a program needn't handle non-finite values.
Results may differ from a plain program's by a relative error of at most 0.0003.
Values sent between devices are 32-bit elements; how exact they have to be, the bound alone decides.
A program may use at most 64 MiB of HBM per device.

v0:
```python
import jax
import jax.numpy as jnp
from jax import lax
from jax.sharding import PartitionSpec as P

LEAF = 512
R = 128
PRB = 16
L_DEV = 4
PTS_DEV = 2048


EXACT_MATMUL = lax.Precision.HIGHEST
SHARPNESS = 2.0
OUTPUT_SCALE = 0.25
NOISE_VAR = 0.5


def kernel_block(left_pts, right_pts):
    distance = jnp.zeros((left_pts.shape[1], right_pts.shape[1]), jnp.float32)
    for coord in range(left_pts.shape[0]):
        differ = left_pts[coord][:, None] - right_pts[coord][None, :]
        distance = distance + differ * differ
    return jnp.exp(-SHARPNESS * distance)


def couple_pairs(current, coupling):
    to_left = jnp.einsum("npr,nrs->nps", current[1::2], coupling, precision=EXACT_MATMUL)
    to_right = jnp.einsum("npr,nsr->nps", current[0::2], coupling, precision=EXACT_MATMUL)
    return jnp.stack([to_left, to_right], axis=1).reshape(current.shape)


def select_columns(values, target_keys, source_keys):
    column_total = target_keys.shape[0]
    block_cols = min(512, column_total)
    block_total = column_total // block_cols
    key_blocks = target_keys.reshape(block_total, block_cols)

    def match_block(keys):
        selector = (keys[:, None] == source_keys[None, :]).astype(jnp.float32)
        return jnp.einsum("ps,ts->pt", values, selector, precision=EXACT_MATMUL)

    stacked = lax.map(match_block, key_blocks)
    return stacked.transpose(1, 0, 2).reshape(values.shape[0], column_total)


def group_ranks(home_device):
    column_total = home_device.shape[0]
    block_cols = min(512, column_total)
    block_total = column_total // block_cols
    places = jnp.arange(column_total, dtype=jnp.int32)

    def rank_block(pieces):
        home_part, place_part = pieces
        matches = (home_part[:, None] == home_device[None, :]) & (
            place_part[:, None] > places[None, :]
        )
        return jnp.sum(matches.astype(jnp.int32), axis=1)

    ranked = lax.map(
        rank_block,
        (home_device.reshape(block_total, block_cols), places.reshape(block_total, block_cols)),
    )
    return ranked.reshape(column_total)


def body(probes, perm, points, anchors, trans_low, couple_low, trans_top, couple_top):
    leaf_count = lax.axis_size("leaf")
    local_levels = L_DEV.bit_length() - 1
    top_levels = leaf_count.bit_length() - 1
    position = lax.axis_index("leaf")
    block_len = PTS_DEV // leaf_count
    spots = points.reshape(points.shape[0], L_DEV, LEAF).transpose(1, 0, 2)
    centres = anchors.reshape(anchors.shape[0], L_DEV, R).transpose(1, 0, 2)
    dense_blocks = jax.vmap(kernel_block)(spots, spots)
    leaf_generator = jax.vmap(kernel_block)(spots, centres)
    home_device = perm // PTS_DEV
    offset = perm - home_device * PTS_DEV
    slot_index = home_device * block_len + group_ranks(home_device)
    places = jnp.arange(PTS_DEV, dtype=jnp.int32)
    wanted_vals = select_columns(offset.astype(jnp.float32)[None, :], places, slot_index)
    wanted = wanted_vals[0].astype(jnp.int32).reshape(leaf_count, block_len)
    asked_rows = lax.all_to_all(wanted, "leaf", split_axis=0, concat_axis=0, tiled=True)
    asked_flat = asked_rows.reshape(-1)
    picked = select_columns(probes, asked_flat, places).reshape(PRB, leaf_count, block_len)
    arrived = lax.all_to_all(picked, "leaf", split_axis=1, concat_axis=1, tiled=True)
    rows_now = arrived.shape[0]
    sorted_vals = arrived.reshape(rows_now, PTS_DEV)
    in_leaves = select_columns(sorted_vals, slot_index, places)
    clustered_rows = in_leaves.reshape(rows_now, L_DEV, LEAF)
    near_field = jnp.einsum("plm,lmn->pln", clustered_rows, dense_blocks, precision=EXACT_MATMUL)
    expansion_weights = jnp.einsum(
        "hks,ksg->hkg", clustered_rows, leaf_generator, precision=EXACT_MATMUL
    )
    clustered_rows, near_field, expansion_weights = (clustered_rows, near_field, expansion_weights)
    ascent = [expansion_weights.transpose(1, 0, 2)]
    for height in range(local_levels):
        node_total = L_DEV >> height
        node_start = sum((L_DEV >> lower for lower in range(height)))
        transfer = trans_low[0, node_start : node_start + node_total].astype(jnp.float32)
        moved = jnp.einsum("npr,nrs->nps", ascent[-1], transfer, precision=EXACT_MATMUL)
        ascent.append(moved.reshape(-1, 2, PRB, R).sum(axis=1))
    summit = ascent[-1][0]
    gathered = lax.all_gather(summit[None], "leaf", axis=0, tiled=True)
    top_ascent = [gathered]
    for upper in range(top_levels - 1):
        node_total = leaf_count >> upper
        node_start = sum((leaf_count >> lower for lower in range(upper)))
        transfer = trans_top[node_start : node_start + node_total].astype(jnp.float32)
        moved = jnp.einsum("npr,nrs->nps", top_ascent[-1], transfer, precision=EXACT_MATMUL)
        top_ascent.append(moved.reshape(-1, 2, PRB, R).sum(axis=1))
    top_descent = None
    for upper in range(top_levels - 1, -1, -1):
        current = top_ascent[upper]
        pair_count = leaf_count >> upper + 1
        pair_start = sum((leaf_count >> lower + 1 for lower in range(upper)))
        coupling = couple_top[pair_start : pair_start + pair_count].astype(jnp.float32)
        coupled = couple_pairs(current, coupling)
        if top_descent is None:
            top_descent = coupled
        else:
            node_total = leaf_count >> upper
            node_start = sum((leaf_count >> lower for lower in range(upper)))
            transfer = trans_top[node_start : node_start + node_total].astype(jnp.float32)
            parents = jnp.repeat(top_descent, 2, axis=0)
            top_descent = coupled + jnp.einsum(
                "npr,nsr->nps", parents, transfer, precision=EXACT_MATMUL
            )
    descending = lax.dynamic_slice_in_dim(top_descent, position, 1, 0)[0]
    downward_sweep = descending[None]
    for height in range(local_levels - 1, -1, -1):
        current = ascent[height]
        pair_count = L_DEV >> height + 1
        pair_start = sum((L_DEV >> lower + 1 for lower in range(height)))
        coupling = couple_low[0, pair_start : pair_start + pair_count].astype(jnp.float32)
        coupled = couple_pairs(current, coupling)
        node_total = L_DEV >> height
        node_start = sum((L_DEV >> lower for lower in range(height)))
        transfer = trans_low[0, node_start : node_start + node_total].astype(jnp.float32)
        parents = jnp.repeat(downward_sweep, 2, axis=0)
        downward_sweep = coupled + jnp.einsum(
            "npr,nsr->nps", parents, transfer, precision=EXACT_MATMUL
        )
    distant_interaction = jnp.einsum(
        "aoj,anj->oan", downward_sweep, leaf_generator, precision=EXACT_MATMUL
    )
    result = OUTPUT_SCALE * (near_field + distant_interaction) + NOISE_VAR * clustered_rows
    outgoing = select_columns(result.reshape(PRB, PTS_DEV), places, slot_index).reshape(
        PRB, leaf_count, block_len
    )
    returned = lax.all_to_all(outgoing, "leaf", split_axis=1, concat_axis=1, tiled=True)
    return select_columns(returned.reshape(PRB, PTS_DEV), places, asked_flat)


def solution(mesh):
    placed = (
        P("probe", "leaf"),
        P("leaf"),
        P(None, "leaf"),
        P(None, "leaf"),
        P("leaf", None, None, None),
        P("leaf", None, None, None),
        P(),
        P(),
    )
    return jax.shard_map(
        body, mesh=mesh, in_specs=placed, out_specs=P("probe", "leaf"), check_vma=False
    )
```

profile of v0, /device:TPU:1, one launch (start us, length us, event | category | flops | bytes accessed | tf_op | source)
XLA Modules:
  0.0 185.1 jit_solution(14503358053438056598)
XLA Ops:
  0.0 0.8 add_select_fusion
  0.8 4.6 %while.66 = (s32[]{:T(128)}, s32[4,512]{1,0:T(4,128)S(1)}, s32[4,512]{1,0:T(4,128)S(1)}, s32[2048]{0:T(1024)S(1)}, s32[4,512]{1,0:T(4,128)S(1)}, /*index=5*/s32[]{:T(128)}, s32[]{:T(128)}) while((s32[]{:T(128)}, s32[4,512]{1,0:T(4,128)S(1)}, s32[4,512]{1,0:T(4,128)S(1)}, s32[2048]{0:T(1024)S(1)}, s32[4,512]{1,0:T(4,128)S(1)}, ...), condition=%wide.region_2.3_spmd.clone, body=%wide.region_0.2_spmd.clone.sunk | while | flops 5242370 | bytes 26709 | solution.py:60
  0.8 1.1 convert_reduce_fusion.3
  2.0 1.1 convert_reduce_fusion.3
  3.1 1.1 convert_reduce_fusion.3
  4.3 1.1 convert_reduce_fusion.3
  5.4 0.7 subtract_convert_fusion
  6.1 7.6 %while.64 = (s32[]{:T(128)}, f32[4,1,512]{2,1,0:T(1,128)S(1)}, s32[4,512]{1,0:T(4,128)S(1)}, s32[2048]{0:T(1024)S(1)}, f32[1,2048]{1,0:T(1,128)S(1)}, /*index=5*/s32[]{:T(128)}) while((s32[]{:T(128)}, f32[4,1,512]{2,1,0:T(1,128)S(1)}, s32[4,512]{1,0:T(4,128)S(1)}, s32[2048]{0:T(1024)S(1)}, f32[1,2048]{1,0:T(1,128)S(1)}, ...), condition=%wide.region_4.5_spmd, body=%wide.region_3.4_spmd.sunk | while | flops 13631490 | bytes 24653 | solution.py:43
  6.1 1.9 %fusion.187 = f32[4,1,512]{2,1,0:T(1,128)S(1)} fusion(f32[4,1,512]{2,1,0:T(1,128)S(1)} %get-tuple-element.508, s32[]{:T(128)} %get-tuple-element.507, s32[2048]{0:T(1024)S(1)} %get-tuple-element.516, s32[512]{0:T(512)S(1)} %bitcast.286, f32[1,2048]{1,0:T(1,128)S(1)} %get-tuple-element.517), kind=kOutput, calls=%fused_computation.8.clone.1 | convolution fusion | flops 13631488 | bytes 20484 | tf_op jit(solution)/shard_map/while/body/eval_jaxpr/ps,ts->pt/dot_general | solution.py:41
  8.0 1.9 %fusion.187 = f32[4,1,512]{2,1,0:T(1,128)S(1)} fusion(f32[4,1,512]{2,1,0:T(1,128)S(1)} %get-tuple-element.508, s32[]{:T(128)} %get-tuple-element.507, s32[2048]{0:T(1024)S(1)} %get-tuple-element.516, s32[512]{0:T(512)S(1)} %bitcast.286, f32[1,2048]{1,0:T(1,128)S(1)} %get-tuple-element.517), kind=kOutput, calls=%fused_computation.8.clone.1 | convolution fusion | flops 13631488 | bytes 20484 | tf_op jit(solution)/shard_map/while/body/eval_jaxpr/ps,ts->pt/dot_general | solution.py:41
  9.9 1.9 %fusion.187 = f32[4,1,512]{2,1,0:T(1,128)S(1)} fusion(f32[4,1,512]{2,1,0:T(1,128)S(1)} %get-tuple-element.508, s32[]{:T(128)} %get-tuple-element.507, s32[2048]{0:T(1024)S(1)} %get-tuple-element.516, s32[512]{0:T(512)S(1)} %bitcast.286, f32[1,2048]{1,0:T(1,128)S(1)} %get-tuple-element.517), kind=kOutput, calls=%fused_computation.8.clone.1 | convolution fusion | flops 13631488 | bytes 20484 | tf_op jit(solution)/shard_map/while/body/eval_jaxpr/ps,ts->pt/dot_general | solution.py:41
  11.8 1.9 %fusion.187 = f32[4,1,512]{2,1,0:T(1,128)S(1)} fusion(f32[4,1,512]{2,1,0:T(1,128)S(1)} %get-tuple-element.508, s32[]{:T(128)} %get-tuple-element.507, s32[2048]{0:T(1024)S(1)} %get-tuple-element.516, s32[512]{0:T(512)S(1)} %bitcast.286, f32[1,2048]{1,0:T(1,128)S(1)} %get-tuple-element.517), kind=kOutput, calls=%fused_computation.8.clone.1 | convolution fusion | flops 13631488 | bytes 20484 | tf_op jit(solution)/shard_map/while/body/eval_jaxpr/ps,ts->pt/dot_general | solution.py:41
  13.8 0.7 convert_element_type.23
  14.5 13.0 %all-to-all-start = ((s32[64,1,32]{2,1,0:T(1,128)}), s32[64,1,32]{2,1,0:T(1,128)S(1)}, u32[]{:S(2)}, u32[]{:S(2)}) async-start(s32[64,1,32]{2,1,0:T(1,128)} %bitcast.12), calls=%async_computation | async-start | bytes 65536 | tf_op jit(solution)/shard_map/all_to_all | solution.py:83
  27.5 9.2 %all-to-all-done = s32[64,1,32]{2,1,0:T(1,128)S(1)} async-done(((s32[64,1,32]{2,1,0:T(1,128)}), s32[64,1,32]{2,1,0:T(1,128)S(1)}, u32[]{:S(2)}, u32[]{:S(2)}) %all-to-all-start) | async-done | bytes 8224 | tf_op jit(solution)/shard_map/all_to_all | solution.py:83
  36.7 0.5 broadcast.32
  37.2 0.7 reduce.7
  38.0 8.2 %while.67 = (s32[]{:T(128)}, f32[4,16,512]{2,1,0:T(8,128)S(1)}, s32[4,512]{1,0:T(4,128)S(1)}, f32[16,2048]{1,0:T(8,128)S(1)}, s32[]{:T(128)}) while((s32[]{:T(128)}, f32[4,16,512]{2,1,0:T(8,128)S(1)}, s32[4,512]{1,0:T(4,128)S(1)}, f32[16,2048]{1,0:T(8,128)S(1)}, s32[]{:T(128)}) %tuple.129), condition=%wide.region_6.7_spmd.clone, body=%wide.region_5.6_spmd.clone.sunk | while | flops 202375168 | bytes 170053 | solution.py:43
  38.1 2.0 %fusion.192 = f32[4,16,512]{2,1,0:T(8,128)S(1)} fusion(f32[4,16,512]{2,1,0:T(8,128)S(1)} %get-tuple-element.525, s32[]{:T(128)} %get-tuple-element.524, f32[16,2048]{1,0:T(8,128)S(1)} %get-tuple-element.532, s32[512]{0:T(512)S(1)} %bitcast.287), kind=kOutput, calls=%fused_computation.34.clone.1 | convolution fusion | flops 202375168 | bytes 165892 | tf_op jit(solution)/shard_map/while/body/eval_jaxpr/ps,ts->pt/dot_general | solution.py:41
  40.1 2.0 %fusion.192 = f32[4,16,512]{2,1,0:T(8,128)S(1)} fusion(f32[4,16,512]{2,1,0:T(8,128)S(1)} %get-tuple-element.525, s32[]{:T(128)} %get-tuple-element.524, f32[16,2048]{1,0:T(8,128)S(1)} %get-tuple-element.532, s32[512]{0:T(512)S(1)} %bitcast.287), kind=kOutput, calls=%fused_computation.34.clone.1 | convolution fusion | flops 202375168 | bytes 165892 | tf_op jit(solution)/shard_map/while/body/eval_jaxpr/ps,ts->pt/dot_general | solution.py:41
  42.2 2.0 %fusion.192 = f32[4,16,512]{2,1,0:T(8,128)S(1)} fusion(f32[4,16,512]{2,1,0:T(8,128)S(1)} %get-tuple-element.525, s32[]{:T(128)} %get-tuple-element.524, f32[16,2048]{1,0:T(8,128)S(1)} %get-tuple-element.532, s32[512]{0:T(512)S(1)} %bitcast.287), kind=kOutput, calls=%fused_computation.34.clone.1 | convolution fusion | flops 202375168 | bytes 165892 | tf_op jit(solution)/shard_map/while/body/eval_jaxpr/ps,ts->pt/dot_general | solution.py:41
  44.2 2.0 %fusion.192 = f32[4,16,512]{2,1,0:T(8,128)S(1)} fusion(f32[4,16,512]{2,1,0:T(8,128)S(1)} %get-tuple-element.525, s32[]{:T(128)} %get-tuple-element.524, f32[16,2048]{1,0:T(8,128)S(1)} %get-tuple-element.532, s32[512]{0:T(512)S(1)} %bitcast.287), kind=kOutput, calls=%fused_computation.34.clone.1 | convolution fusion | flops 202375168 | bytes 165892 | tf_op jit(solution)/shard_map/while/body/eval_jaxpr/ps,ts->pt/dot_general | solution.py:41
  46.8 0.9 reshape.248
  47.8 4.7 %all-to-all-start.1 = ((f32[64,1,512]{2,1,0:T(1,128)}), f32[64,1,512]{2,1,0:T(1,128)S(1)}, u32[]{:S(2)}, u32[]{:S(2)}) async-start(f32[64,1,512]{2,1,0:T(1,128)} %reshape.248), calls=%async_computation.1 | async-start | bytes 262144 | tf_op jit(solution)/shard_map/all_to_all | solution.py:86
  52.6 10.4 %all-to-all-done.1 = f32[64,1,512]{2,1,0:T(1,128)S(1)} async-done(((f32[64,1,512]{2,1,0:T(1,128)}), f32[64,1,512]{2,1,0:T(1,128)S(1)}, u32[]{:S(2)}, u32[]{:S(2)}) %all-to-all-start.1) | async-done | bytes 131104 | tf_op jit(solution)/shard_map/all_to_all | solution.py:86
  63.0 0.6 broadcast.33
  63.5 0.9 reduce.8
  65.1 8.2 %while.68 = (s32[]{:T(128)}, f32[4,16,512]{2,1,0:T(8,128)S(1)}, s32[4,512]{1,0:T(4,128)S(1)}, f32[16,2048]{1,0:T(8,128)S(1)}, s32[]{:T(128)}) while((s32[]{:T(128)}, f32[4,16,512]{2,1,0:T(8,128)S(1)}, s32[4,512]{1,0:T(4,128)S(1)}, f32[16,2048]{1,0:T(8,128)S(1)}, s32[]{:T(128)}) %tuple.113), condition=%wide.region_8.9_spmd.clone, body=%wide.region_7.8_spmd.clone.sunk | while | flops 202375168 | bytes 170053 | solution.py:43
  65.1 2.0 %fusion.194 = f32[4,16,512]{2,1,0:T(8,128)S(1)} fusion(f32[4,16,512]{2,1,0:T(8,128)S(1)} %get-tuple-element.540, s32[]{:T(128)} %get-tuple-element.539, f32[16,2048]{1,0:T(8,128)S(1)} %get-tuple-element.547, s32[512]{0:T(512)S(1)} %bitcast.288), kind=kOutput, calls=%fused_computation.40.clone.1 | convolution fusion | flops 202375168 | bytes 165892 | tf_op jit(solution)/shard_map/while/body/eval_jaxpr/ps,ts->pt/dot_general | solution.py:41
  67.2 2.0 %fusion.194 = f32[4,16,512]{2,1,0:T(8,128)S(1)} fusion(f32[4,16,512]{2,1,0:T(8,128)S(1)} %get-tuple-element.540, s32[]{:T(128)} %get-tuple-element.539, f32[16,2048]{1,0:T(8,128)S(1)} %get-tuple-element.547, s32[512]{0:T(512)S(1)} %bitcast.288), kind=kOutput, calls=%fused_computation.40.clone.1 | convolution fusion | flops 202375168 | bytes 165892 | tf_op jit(solution)/shard_map/while/body/eval_jaxpr/ps,ts->pt/dot_general | solution.py:41
  69.2 2.0 %fusion.194 = f32[4,16,512]{2,1,0:T(8,128)S(1)} fusion(f32[4,16,512]{2,1,0:T(8,128)S(1)} %get-tuple-element.540, s32[]{:T(128)} %get-tuple-element.539, f32[16,2048]{1,0:T(8,128)S(1)} %get-tuple-element.547, s32[512]{0:T(512)S(1)} %bitcast.288), kind=kOutput, calls=%fused_computation.40.clone.1 | convolution fusion | flops 202375168 | bytes 165892 | tf_op jit(solution)/shard_map/while/body/eval_jaxpr/ps,ts->pt/dot_general | solution.py:41
  71.3 2.0 %fusion.194 = f32[4,16,512]{2,1,0:T(8,128)S(1)} fusion(f32[4,16,512]{2,1,0:T(8,128)S(1)} %get-tuple-element.540, s32[]{:T(128)} %get-tuple-element.539, f32[16,2048]{1,0:T(8,128)S(1)} %get-tuple-element.547, s32[512]{0:T(512)S(1)} %bitcast.288), kind=kOutput, calls=%fused_computation.40.clone.1 | convolution fusion | flops 202375168 | bytes 165892 | tf_op jit(solution)/shard_map/while/body/eval_jaxpr/ps,ts->pt/dot_general | solution.py:41
  73.3 2.0 %fusion.72 = f32[4,128,16]{1,2,0:T(8,128)S(1)} fusion(f32[4,128]{1,0:T(4,128)S(1)} %get-tuple-element.274, f32[4,512]{1,0:T(4,128)S(1)} %get-tuple-element.269, f32[4,128]{1,0:T(4,128)S(1)} %get-tuple-element.275, f32[4,512]{1,0:T(4,128)S(1)} %get-tuple-element.270, f32[4,128]{1,0:T(4,128)S(1)} %get-tuple-element.273, f32[4,512]{1,0:T(4,128)S(1)} %get-tuple-element.268, ...), kind=kOutput, calls=%fused_computation.93 | convolution fusion | flops 52690944 | bytes 194560 | tf_op jit(solution)/shard_map/hks,ksg->hkg/dot_general | solution.py:92
  75.7 48.9 %all-gather = f32[1024,128]{1,0:T(8,128)S(1)} all-gather(f32[16,128]{1,0:T(8,128)S(1)} %convolution_bitcast_fusion.14), channel_id=2, replica_groups=mesh['leaf'=64,'probe'=4] {'leaf'}, dimensions={0}, use_global_device_ids=true | all-gather | bytes 532480 | tf_op jit(solution)/shard_map/all_gather | solution.py:104
  124.5 1.7 convolution_bitcast_fusion
  126.3 0.9 convolution_bitcast_fusion.1
  127.2 1.7 bitcast_reduce_fusion
  129.0 0.9 bitcast_reduce_fusion.1
  129.9 0.5 bitcast_reduce_fusion.2
  132.2 0.5 convolution_bitcast_fusion.4
  132.7 0.3 convolution_bitcast_fusion.5
  133.1 0.9 convolution_bitcast_fusion.2
  134.0 0.5 convolution_bitcast_fusion.3
  135.2 4.5 %fusion.46 = f32[4,512,16]{1,2,0:T(8,128)S(1)} fusion(f32[4,512]{1,0:T(4,128)S(1)} %get-tuple-element.269, f32[4,512]{1,0:T(4,128)S(1)} %get-tuple-element.270, f32[4,512]{1,0:T(4,128)S(1)} %get-tuple-element.268, f32[4,16,512]{2,1,0:T(8,128)S(1)} %get-tuple-element.175), kind=kOutput, calls=%fused_computation.42 | convolution fusion | flops 210763776 | bytes 286720 | tf_op jit(solution)/shard_map/plm,lmn->pln/dot_general | solution.py:91
  140.4 0.5 convolution_add_fusion.3
  140.9 0.9 convolution_add_fusion.1
  141.8 1.7 convolution_add_fusion
  143.6 3.3 %fusion.64 = f32[64,16,128]{2,1,0:T(8,128)S(1)} fusion(f32[64,16,128]{2,1,0:T(8,128)S(1)} %bitcast.262, bf16[126,128,128]{2,1,0:T(8,128)(2,1)S(1)} %copy-done), kind=kOutput, calls=%fused_computation.60 | convolution fusion | flops 201326592 | bytes 3145728 | tf_op jit(solution)/shard_map/npr,nsr->nps/dot_general | solution.py:126
  147.5 2.3 %fusion.71 = f32[4,2,8,512]{3,2,1,0:T(8,128)S(1)} fusion(f32[4,512,16]{1,2,0:T(8,128)S(1)} %fusion.46, f32[4,16,128]{2,1,0:T(8,128)S(1)} %convolution_add_fusion.4, f32[4,128]{1,0:T(4,128)S(1)} %get-tuple-element.274, f32[4,512]{1,0:T(4,128)S(1)} %get-tuple-element.269, f32[4,128]{1,0:T(4,128)S(1)} %get-tuple-element.275, ...), kind=kOutput, calls=%fused_computation.74 | convolution fusion | flops 52822016 | bytes 456704 | tf_op jit(solution)/shard_map/aoj,anj->oan/dot_general | solution.py:144
  149.9 7.6 %while.65 = (s32[]{:T(128)}, f32[4,16,512]{2,1,0:T(8,128)S(1)}, s32[4,512]{1,0:T(4,128)S(1)}, s32[2048]{0:T(1024)S(1)}, f32[16,2048]{1,0:T(8,128)S(1)}, /*index=5*/s32[]{:T(128)}) while((s32[]{:T(128)}, f32[4,16,512]{2,1,0:T(8,128)S(1)}, s32[4,512]{1,0:T(4,128)S(1)}, s32[2048]{0:T(1024)S(1)}, f32[16,2048]{1,0:T(8,128)S(1)}, ...), condition=%wide.region_16.17_spmd, body=%wide.region_15.16_spmd.sunk | while | flops 202375168 | bytes 178253 | solution.py:43
  150.0 1.9 %fusion.190 = f32[4,16,512]{2,1,0:T(8,128)S(1)} fusion(f32[4,16,512]{2,1,0:T(8,128)S(1)} %get-tuple-element.556, s32[]{:T(128)} %get-tuple-element.555, f32[16,2048]{1,0:T(8,128)S(1)} %get-tuple-element.565, s32[2048]{0:T(1024)S(1)} %get-tuple-element.564, s32[512]{0:T(512)S(1)} %bitcast.289), kind=kOutput, calls=%fused_computation.16.clone.1 | convolution fusion | flops 202375168 | bytes 174084 | tf_op jit(solution)/shard_map/while/body/eval_jaxpr/ps,ts->pt/dot_general | solution.py:41
  151.9 1.9 %fusion.190 = f32[4,16,512]{2,1,0:T(8,128)S(1)} fusion(f32[4,16,512]{2,1,0:T(8,128)S(1)} %get-tuple-element.556, s32[]{:T(128)} %get-tuple-element.555, f32[16,2048]{1,0:T(8,128)S(1)} %get-tuple-element.565, s32[2048]{0:T(1024)S(1)} %get-tuple-element.564, s32[512]{0:T(512)S(1)} %bitcast.289), kind=kOutput, calls=%fused_computation.16.clone.1 | convolution fusion | flops 202375168 | bytes 174084 | tf_op jit(solution)/shard_map/while/body/eval_jaxpr/ps,ts->pt/dot_general | solution.py:41
  153.8 1.9 %fusion.190 = f32[4,16,512]{2,1,0:T(8,128)S(1)} fusion(f32[4,16,512]{2,1,0:T(8,128)S(1)} %get-tuple-element.556, s32[]{:T(128)} %get-tuple-element.555, f32[16,2048]{1,0:T(8,128)S(1)} %get-tuple-element.565, s32[2048]{0:T(1024)S(1)} %get-tuple-element.564, s32[512]{0:T(512)S(1)} %bitcast.289), kind=kOutput, calls=%fused_computation.16.clone.1 | convolution fusion | flops 202375168 | bytes 174084 | tf_op jit(solution)/shard_map/while/body/eval_jaxpr/ps,ts->pt/dot_general | solution.py:41
  155.7 1.9 %fusion.190 = f32[4,16,512]{2,1,0:T(8,128)S(1)} fusion(f32[4,16,512]{2,1,0:T(8,128)S(1)} %get-tuple-element.556, s32[]{:T(128)} %get-tuple-element.555, f32[16,2048]{1,0:T(8,128)S(1)} %get-tuple-element.565, s32[2048]{0:T(1024)S(1)} %get-tuple-element.564, s32[512]{0:T(512)S(1)} %bitcast.289), kind=kOutput, calls=%fused_computation.16.clone.1 | convolution fusion | flops 202375168 | bytes 174084 | tf_op jit(solution)/shard_map/while/body/eval_jaxpr/ps,ts->pt/dot_general | solution.py:41
  158.2 0.9 reshape.250
  159.1 5.7 %all-to-all-start.2 = ((f32[64,1,512]{2,1,0:T(1,128)}), f32[64,1,512]{2,1,0:T(1,128)S(1)}, u32[]{:S(2)}, u32[]{:S(2)}) async-start(f32[64,1,512]{2,1,0:T(1,128)} %reshape.250), calls=%async_computation.2 | async-start | bytes 262144 | tf_op jit(solution)/shard_map/all_to_all | solution.py:151
  164.9 10.3 %all-to-all-done.2 = f32[64,1,512]{2,1,0:T(1,128)S(1)} async-done(((f32[64,1,512]{2,1,0:T(1,128)}), f32[64,1,512]{2,1,0:T(1,128)S(1)}, u32[]{:S(2)}, u32[]{:S(2)}) %all-to-all-start.2) | async-done | bytes 131104 | tf_op jit(solution)/shard_map/all_to_all | solution.py:151
  175.2 0.9 reduce.9
  176.7 7.6 %while.69 = (s32[]{:T(128)}, f32[4,16,512]{2,1,0:T(8,128)S(1)}, s32[4,512]{1,0:T(4,128)S(1)}, s32[64,32]{1,0:T(8,128)}, f32[16,2048]{1,0:T(8,128)S(1)}, /*index=5*/s32[2048]{0:T(1024)S(1)}, s32[]{:T(128)}) while((s32[]{:T(128)}, f32[4,16,512]{2,1,0:T(8,128)S(1)}, s32[4,512]{1,0:T(4,128)S(1)}, s32[64,32]{1,0:T(8,128)}, ...), condition=%wide.wide.region_18.19_spmd, body=%wide.wide.region_17.18_spmd.sunk | while | flops 202375168 | bytes 178261 | solution.py:43
  176.8 1.9 %fusion.197 = f32[4,16,512]{2,1,0:T(8,128)S(1)} fusion(f32[4,16,512]{2,1,0:T(8,128)S(1)} %get-tuple-element.575, s32[]{:T(128)} %get-tuple-element.574, f32[16,2048]{1,0:T(8,128)S(1)} %get-tuple-element.585, s32[2048]{0:T(1024)S(1)} %get-tuple-element.586, s32[512]{0:T(512)S(1)} %bitcast.290), kind=kOutput, calls=%fused_computation.23.clone.clone.1 | convolution fusion | flops 202375168 | bytes 174084 | tf_op jit(solution)/shard_map/while/body/eval_jaxpr/ps,ts->pt/dot_general | solution.py:41
  178.7 1.9 %fusion.197 = f32[4,16,512]{2,1,0:T(8,128)S(1)} fusion(f32[4,16,512]{2,1,0:T(8,128)S(1)} %get-tuple-element.575, s32[]{:T(128)} %get-tuple-element.574, f32[16,2048]{1,0:T(8,128)S(1)} %get-tuple-element.585, s32[2048]{0:T(1024)S(1)} %get-tuple-element.586, s32[512]{0:T(512)S(1)} %bitcast.290), kind=kOutput, calls=%fused_computation.23.clone.clone.1 | convolution fusion | flops 202375168 | bytes 174084 | tf_op jit(solution)/shard_map/while/body/eval_jaxpr/ps,ts->pt/dot_general | solution.py:41
  180.6 1.9 %fusion.197 = f32[4,16,512]{2,1,0:T(8,128)S(1)} fusion(f32[4,16,512]{2,1,0:T(8,128)S(1)} %get-tuple-element.575, s32[]{:T(128)} %get-tuple-element.574, f32[16,2048]{1,0:T(8,128)S(1)} %get-tuple-element.585, s32[2048]{0:T(1024)S(1)} %get-tuple-element.586, s32[512]{0:T(512)S(1)} %bitcast.290), kind=kOutput, calls=%fused_computation.23.clone.clone.1 | convolution fusion | flops 202375168 | bytes 174084 | tf_op jit(solution)/shard_map/while/body/eval_jaxpr/ps,ts->pt/dot_general | solution.py:41
  182.5 1.9 %fusion.197 = f32[4,16,512]{2,1,0:T(8,128)S(1)} fusion(f32[4,16,512]{2,1,0:T(8,128)S(1)} %get-tuple-element.575, s32[]{:T(128)} %get-tuple-element.574, f32[16,2048]{1,0:T(8,128)S(1)} %get-tuple-element.585, s32[2048]{0:T(1024)S(1)} %get-tuple-element.586, s32[512]{0:T(512)S(1)} %bitcast.290), kind=kOutput, calls=%fused_computation.23.clone.clone.1 | convolution fusion | flops 202375168 | bytes 174084 | tf_op jit(solution)/shard_map/while/body/eval_jaxpr/ps,ts->pt/dot_general | solution.py:41
  184.4 0.7 copy.51
  (111 shorter events, 7.3 us)
Async XLA Ops:
  0.0 27.4 %copy-start.6 = (f32[3,512]{1,0:T(4,128)S(1)}, f32[3,512]{1,0:T(4,128)}, u32[]{:S(2)}) copy-start(f32[3,512]{1,0:T(4,128)} %param.23) | copy-start | bytes 18436
  0.0 38.0 %copy-start.7 = (f32[16,2048]{1,0:T(8,128)S(1)}, f32[16,2048]{1,0:T(8,128)}, u32[]{:S(2)}) copy-start(f32[16,2048]{1,0:T(8,128)} %param.20) | copy-start | bytes 393220
  14.5 22.2 %all-to-all-start = ((s32[64,1,32]{2,1,0:T(1,128)}), s32[64,1,32]{2,1,0:T(1,128)S(1)}, u32[]{:S(2)}, u32[]{:S(2)}) async-start(s32[64,1,32]{2,1,0:T(1,128)} %bitcast.12), calls=%async_computation | async-start | bytes 65536 | tf_op jit(solution)/shard_map/all_to_all | solution.py:83
  36.7 128.2 %copy-start.4 = (s32[64,1,32]{2,1,0:T(1,128)}, s32[64,1,32]{2,1,0:T(1,128)S(1)}, u32[]{:S(2)}) copy-start(s32[64,1,32]{2,1,0:T(1,128)S(1)} %all-to-all-done) | copy-start | bytes 24580
  38.0 14.5 %copy-start.5 = (f32[3,2048]{1,0:T(4,128)S(1)}, f32[3,2048]{1,0:T(4,128)}, u32[]{:S(2)}) copy-start(f32[3,2048]{1,0:T(4,128)} %param.22) | copy-start | bytes 73732
  47.8 15.2 %all-to-all-start.1 = ((f32[64,1,512]{2,1,0:T(1,128)}), f32[64,1,512]{2,1,0:T(1,128)S(1)}, u32[]{:S(2)}, u32[]{:S(2)}) async-start(f32[64,1,512]{2,1,0:T(1,128)} %reshape.248), calls=%async_computation.1 | async-start | bytes 262144 | tf_op jit(solution)/shard_map/all_to_all | solution.py:86
  65.1 10.2 %copy-start.2 = (bf16[1,6,128,128]{3,2,1,0:T(8,128)(2,1)S(1)}, bf16[1,6,128,128]{3,2,1,0:T(8,128)(2,1)}, u32[]{:S(2)}) copy-start(bf16[1,6,128,128]{3,2,1,0:T(8,128)(2,1)} %param.24) | copy-start | bytes 589828
  65.1 59.4 %copy-start.1 = (bf16[63,128,128]{2,1,0:T(8,128)(2,1)S(1)}, bf16[63,128,128]{2,1,0:T(8,128)(2,1)}, u32[]{:S(2)}) copy-start(bf16[63,128,128]{2,1,0:T(8,128)(2,1)} %param.27) | copy-start | bytes 6193156
  73.3 53.9 %copy-start = (bf16[126,128,128]{2,1,0:T(8,128)(2,1)S(1)}, bf16[126,128,128]{2,1,0:T(8,128)(2,1)}, u32[]{:S(2)}) copy-start(bf16[126,128,128]{2,1,0:T(8,128)(2,1)} %param.26) | copy-start | bytes 12386308
  127.2 7.3 %copy-start.3 = (bf16[1,3,128,128]{3,2,1,0:T(8,128)(2,1)S(1)}, bf16[1,3,128,128]{3,2,1,0:T(8,128)(2,1)}, u32[]{:S(2)}) copy-start(bf16[1,3,128,128]{3,2,1,0:T(8,128)(2,1)} %param.25) | copy-start | bytes 294916
  159.1 16.1 %all-to-all-start.2 = ((f32[64,1,512]{2,1,0:T(1,128)}), f32[64,1,512]{2,1,0:T(1,128)S(1)}, u32[]{:S(2)}, u32[]{:S(2)}) async-start(f32[64,1,512]{2,1,0:T(1,128)} %reshape.250), calls=%async_computation.2 | async-start | bytes 262144 | tf_op jit(solution)/shard_map/all_to_all | solution.py:151
where the time goes:
time: 185 us
  matrix products  65.9 us (36%)
  blocking collectives  48.9 us (26%)
  waiting for transfers between devices  29.9 us (16%)
  starting transfers between devices  23.4 us (13%)
  other arithmetic  8.47 us (5%)
  local copies, waits for them, and re-layouts  7.72 us (4%)
    all_gather x1, blocking collectives, body(): gathered = lax.all_gather(summit[None], 'leaf', axis=0, tiled=True)  48.9 us
    dot_general x20, matrix products, match_block(): return jnp.einsum('ps,ts->pt', values, selector, precision=EXACT_MATMUL)  38.8 us
    all_to_all x1, starting transfers between devices, body(): lax.all_to_all(wanted, 'leaf', split_axis=0, concat_axis=0, tiled=True)  13 us
    all_to_all x1, waiting for transfers between devices, body(): lax.all_to_all(picked, 'leaf', split_axis=1, concat_axis=1, tiled=True)  10.4 us
    all_to_all x1, waiting for transfers between devices, body(): lax.all_to_all(outgoing, 'leaf', split_axis=1, concat_axis=1, tiled=True)  10.3 us
    all_to_all x1, waiting for transfers between devices, body(): lax.all_to_all(wanted, 'leaf', split_axis=0, concat_axis=0, tiled=True)  9.19 us
    dot_general x7, matrix products, body(): jnp.einsum('npr,nsr->nps', parents, transfer, precision=EXACT_MATMUL)  7.3 us
    all_to_all x1, starting transfers between devices, body(): lax.all_to_all(outgoing, 'leaf', split_axis=1, concat_axis=1, tiled=True)  5.73 us
  transfers between devices with their start and end apart: 3, of which 3 were waited for; matrix products, arithmetic and copies ran while one was open for 0% of the time, Pallas kernels for 0%

commit v1 on v0

v1 whole, which is shorter than its diff:
```python
import functools

import jax
import jax.numpy as jnp
from jax import lax
from jax.experimental import pallas as pl
from jax.experimental.pallas import tpu as pltpu
from jax.sharding import PartitionSpec as P

LEAF = 512
R = 128
PRB = 16
L_DEV = 4
PTS = 2048
N = 64
BLK = PTS // N
TILES = PTS // 128
SHARPNESS = 2.0
OUTPUT_SCALE = 0.25
NOISE_VAR = 0.5
MESH = pl.DeviceIdType.MESH
F32 = jnp.float32
BF16 = jnp.bfloat16
I32 = jnp.int32


def dot(a, b):
    return jnp.dot(a, b, preferred_element_type=F32)


def dot_nt(a, b):
    return lax.dot_general(a, b, (((1,), (1,)), ((), ())), preferred_element_type=F32)


def split(v):
    hi = v.astype(BF16)
    lo = (v - hi.astype(F32)).astype(BF16)
    return hi, lo


def pair(v):
    hi, lo = split(v)
    return jnp.concatenate([hi, lo], axis=0)


def fold(r):
    return r[:PRB] + r[PRB:]


def iota(shape, dim):
    return lax.broadcasted_iota(I32, shape, dim)


def swap_blocks(tile):
    lane = iota((8, 128), 1)
    row = iota((8, 128), 0)
    v0, v1 = tile[:8], tile[8:]
    low = lane < 64
    a0 = jnp.where(low, v0, pltpu.roll(v1, 64, 1))
    a1 = jnp.where(low, pltpu.roll(v0, 64, 1), v1)
    lane_bit = (lane >> 5) & 1
    same = (row >> 2) == lane_bit
    outs = []
    for a in (a0, a1):
        y = pltpu.roll(a, 4, 0)
        moved = jnp.where(lane_bit == 1, pltpu.roll(y, 32, 1), pltpu.roll(y, 96, 1))
        outs.append(jnp.where(same, a, moved))
    return outs


def gather_tile(source, index_row):
    index = jnp.broadcast_to(index_row, (8, 128))
    lane = index & 127
    tile = index >> 7
    out0 = jnp.zeros((8, 128), F32)
    out1 = jnp.zeros((8, 128), F32)
    for s in range(TILES):
        v = source(s)
        here = tile == s
        g0 = jnp.take_along_axis(v[:8], lane, axis=1, mode="promise_in_bounds")
        g1 = jnp.take_along_axis(v[8:], lane, axis=1, mode="promise_in_bounds")
        out0 = jnp.where(here, g0, out0)
        out1 = jnp.where(here, g1, out1)
    return jnp.concatenate([out0, out1], axis=0)


def by_lane_block(rows):
    block = iota((1, 128), 1) >> 5
    out = rows[3]
    for b in (2, 1, 0):
        out = jnp.where(block == b, rows[b], out)
    return out


def kernel(
    perm_h, points_h, anchors_h, probes_h, tl_h, cl_h, tt_h, ct_h,
    out_v,
    perm_v, points_v, anchors_v, probes_v, tl_v, cl_v,
    e0_v, e1_v, e2_v, e3_v, e4_v, ct_v, cs_v,
    slot_v, inv_v, asked_v, back_v,
    ptst_v, dhi_v, dlo_v, bhi_v, blo_v,
    x_v, x2_v, xs_v, y_v, near_v,
    idx_s, idx_r, a_s, a_r, b_s, b_r,
    q0_v, q1_v, q2_v, q3_v, q4_v, q5_v,
    load_sem, send_sem, recv_sem, own_sem,
):
    me = lax.axis_index("leaf")
    group = me // 8
    pos = me % 8

    loads = [
        pltpu.make_async_copy(perm_h, perm_v, load_sem.at[0]),
        pltpu.make_async_copy(points_h, points_v.at[pl.ds(0, 3)], load_sem.at[1]),
        pltpu.make_async_copy(anchors_h, anchors_v, load_sem.at[2]),
        pltpu.make_async_copy(probes_h, probes_v, load_sem.at[3]),
        pltpu.make_async_copy(tl_h.at[0], tl_v, load_sem.at[4]),
        pltpu.make_async_copy(cl_h.at[0], cl_v, load_sem.at[5]),
        pltpu.make_async_copy(tt_h.at[pl.ds(group * 8, 8)], e0_v, load_sem.at[6]),
        pltpu.make_async_copy(tt_h.at[pl.ds(64 + group * 4, 4)], e1_v, load_sem.at[7]),
        pltpu.make_async_copy(tt_h.at[pl.ds(96 + group * 2, 2)], e2_v, load_sem.at[8]),
        pltpu.make_async_copy(tt_h.at[pl.ds(112, 8)], e3_v, load_sem.at[9]),
        pltpu.make_async_copy(tt_h.at[pl.ds(120, 4)], e4_v, load_sem.at[10]),
    ]
    for t, start in enumerate((0, 32, 48, 56, 60, 62)):
        loads.append(
            pltpu.make_async_copy(
                ct_h.at[pl.ds(start + me // (2 << t), 1)], ct_v.at[pl.ds(t, 1)], load_sem.at[11 + t]
            )
        )
    for copy in loads:
        copy.start()

    barrier = pltpu.get_barrier_semaphore()

    @pl.loop(1, N)
    def _(k):
        pl.semaphore_signal(barrier, inc=1, device_id={"leaf": (me + k) % N}, device_id_type=MESH)

    def remote(src, dst, which, peer):
        return pltpu.make_async_remote_copy(
            src_ref=src, dst_ref=dst, send_sem=send_sem.at[which], recv_sem=recv_sem.at[which],
            device_id={"leaf": peer}, device_id_type=MESH,
        )

    loads[0].wait()
    row64 = iota((N, 128), 0)
    lane1 = iota((1, 128), 1)
    ones = []
    for b in range(TILES):
        home = perm_v[b : b + 1, :] >> 11
        ones.append((row64 == home).astype(F32))
    before = (iota((128, 128), 0) < iota((128, 128), 1)).astype(BF16)
    counter = jnp.concatenate([before, jnp.ones((128, 128), BF16)], axis=1)
    counts = dot(jnp.concatenate(ones, axis=0).astype(BF16), counter)
    base = jnp.zeros((N, 128), F32)
    found = jnp.zeros((4 * N, 128), F32)
    row128 = iota((128, 128), 0) & (BLK - 1)
    for b in range(TILES):
        entry = perm_v[b : b + 1, :]
        one = ones[b]
        rank = jnp.sum(one * (counts[N * b : N * (b + 1), :128] + base), axis=0, keepdims=True)
        base = base + counts[N * b : N * (b + 1), 128:]
        rank = rank.astype(I32)
        slot_v[b : b + 1, :] = (entry >> 11) * BLK + rank
        offset = entry & (PTS - 1)
        left = jnp.concatenate(
            [
                one * (offset >> 8).astype(F32),
                one * (offset & 255).astype(F32),
                one * float(b),
                one * lane1.astype(F32),
            ],
            axis=0,
        ).astype(BF16)
        right = (row128 == rank).astype(F32).astype(BF16)
        found = found + dot_nt(left, right)
    wanted = (found[:N] * 256.0 + found[N : 2 * N]).astype(I32)
    places = (found[2 * N : 3 * N] * 128.0 + found[3 * N :]).astype(I32)
    for h in range(N):
        idx_s[h] = wanted[h : h + 1, :]
    for o in range(TILES):
        inv_v[o : o + 1, :] = by_lane_block([places[4 * o + b : 4 * o + b + 1, :] for b in range(4)])

    pl.semaphore_wait(barrier, N - 1)

    @pl.loop(1, N)
    def _(k):
        peer = (me + k) % N
        remote(idx_s.at[peer], idx_r.at[me], 0, peer).start()

    own = pltpu.make_async_copy(idx_s.at[me], idx_r.at[me], own_sem.at[0])
    own.start()

    loads[1].wait()
    loads[2].wait()
    for b in range(TILES):
        ptst_v[128 * b : 128 * (b + 1), :] = jnp.transpose(points_v[:, 128 * b : 128 * (b + 1)])

    rows = 64

    @pl.loop(0, PTS // rows)
    def _(i):
        at = pl.ds(pl.multiple_of(i * rows, rows), rows)
        leaf = i // (LEAF // rows)
        total = None
        for c in range(3):
            left = ptst_v[at, c : c + 1]
            right = anchors_v[c : c + 1, pl.ds(pl.multiple_of(leaf * R, R), R)]
            differ = left - right
            total = differ * differ if total is None else total + differ * differ
        hi, lo = split(jnp.exp(-SHARPNESS * total))
        bhi_v[at, :] = hi
        blo_v[at, :] = lo

    own.wait()
    remote(idx_s.at[pl.ds(0, N - 1)], idx_r.at[pl.ds(0, N - 1)], 0, me).wait()

    for o in range(TILES):
        asked_v[o : o + 1, :] = by_lane_block([idx_r[4 * o + b] for b in range(4)])

    loads[3].wait()

    def send_tile(tile, o, s_ref, r_ref, which, own_at):
        halves = swap_blocks(tile)
        for h in range(4):
            s_ref[4 * o + h] = halves[h // 2][4 * (h % 2) : 4 * (h % 2) + 4]
        for h in range(4):
            peer = 4 * o + h

            @pl.when(peer != me)
            def _():
                remote(s_ref.at[peer], r_ref.at[me], which, peer).start()

            @pl.when(peer == me)
            def _():
                pltpu.make_async_copy(s_ref.at[peer], r_ref.at[me], own_sem.at[own_at]).start()

    def receive_tiles(s_ref, r_ref, which, own_at):
        pltpu.make_async_copy(s_ref.at[me], r_ref.at[me], own_sem.at[own_at]).wait()
        remote(s_ref.at[pl.ds(0, N - 1)], r_ref.at[pl.ds(0, N - 1)], which, me).wait()

        @pl.loop(0, TILES)
        def _(o):
            parts = [r_ref[4 * o + h] for h in range(4)]
            both = jnp.concatenate(parts, axis=0)
            out = swap_blocks(both)
            xs_v[o] = jnp.concatenate(out, axis=0)

    @pl.loop(0, TILES)
    def _(i):
        o = (me // 4 + i) % TILES
        tile = gather_tile(lambda s: probes_v[:, 128 * s : 128 * (s + 1)], asked_v[pl.ds(o, 1), :])
        send_tile(tile, o, a_s, a_r, 1, 1)

    drows = 32

    @pl.loop(0, PTS // drows)
    def _(i):
        at = pl.ds(pl.multiple_of(i * drows, drows), drows)
        leaf = i // (LEAF // drows)
        total = None
        for c in range(3):
            left = ptst_v[at, c : c + 1]
            right = points_v[c : c + 1, pl.ds(pl.multiple_of(leaf * LEAF, LEAF), LEAF)]
            differ = left - right
            total = differ * differ if total is None else total + differ * differ
        hi, lo = split(jnp.exp(-SHARPNESS * total))
        dhi_v[at, :] = hi
        dlo_v[at, :] = lo

    found = jnp.zeros((2 * TILES, 128), F32)
    row16 = iota((TILES, 128), 0)
    row128 = iota((128, 128), 0)
    for o in range(TILES):
        asked = asked_v[o : o + 1, :]
        one = (row16 == (asked >> 7)).astype(F32)
        left = jnp.concatenate([one * float(o), one * lane1.astype(F32)], axis=0).astype(BF16)
        right = (row128 == (asked & 127)).astype(F32).astype(BF16)
        found = found + dot_nt(left, right)
    back_v[...] = (found[:TILES] * 128.0 + found[TILES:]).astype(I32)

    for copy in loads[4:]:
        copy.wait()
    for t in range(6):
        mat = ct_v[t].astype(F32)
        odd = (me // (1 << t)) % 2
        cs_v[t] = jnp.where(odd == 1, jnp.transpose(mat), mat).astype(BF16)

    receive_tiles(a_s, a_r, 1, 1)

    @pl.loop(0, TILES)
    def _(o):
        tile = gather_tile(lambda s: xs_v[s], slot_v[pl.ds(o, 1), :])
        at = pl.ds(pl.multiple_of(o * 128, 128), 128)
        x_v[:, at] = tile
        x2_v[:, at] = pair(tile)

    def up(children, transfers):
        lhs = pair(jnp.concatenate(children, axis=1))
        return fold(dot(lhs, transfers.reshape(2 * R, R)))

    leaves = []
    for i in range(L_DEV):
        x2 = x2_v[:, LEAF * i : LEAF * (i + 1)]
        at = slice(LEAF * i, LEAF * (i + 1))
        leaves.append(fold(dot(x2, bhi_v[at, :])) + dot(x2[:PRB], blo_v[at, :]))
    mids = [up(leaves[2 * n : 2 * n + 2], tl_v[2 * n : 2 * n + 2]) for n in range(2)]
    q0_v[pos] = up(mids, tl_v[4:6])

    @pl.loop(1, 8)
    def _(k):
        peer = group * 8 + (pos + k) % 8
        remote(q0_v.at[pos], q0_v.at[pos], 2, peer).start()

    def near(i):
        x2 = x2_v[:, LEAF * i : LEAF * (i + 1)]
        at = slice(LEAF * i, LEAF * (i + 1))
        near_v[:, at] = fold(dot(x2, dhi_v[at, :])) + dot(x2[:PRB], dlo_v[at, :])

    near(0)
    near(1)
    remote(q0_v.at[pl.ds(0, 7)], q0_v.at[pl.ds(0, 7)], 2, me).wait()
    for n in range(4):
        q1_v[n] = up([q0_v[2 * n], q0_v[2 * n + 1]], e0_v[2 * n : 2 * n + 2])
    for n in range(2):
        q2_v[n] = up([q1_v[2 * n], q1_v[2 * n + 1]], e1_v[2 * n : 2 * n + 2])
    q3_v[group] = up([q2_v[0], q2_v[1]], e2_v[...])

    @pl.loop(1, 8)
    def _(k):
        peer = ((group + k) % 8) * 8 + pos
        remote(q3_v.at[group], q3_v.at[group], 3, peer).start()

    near(2)
    near(3)
    remote(q3_v.at[pl.ds(0, 7)], q3_v.at[pl.ds(0, 7)], 3, me).wait()
    for n in range(4):
        q4_v[n] = up([q3_v[2 * n], q3_v[2 * n + 1]], e3_v[2 * n : 2 * n + 2])
    for n in range(2):
        q5_v[n] = up([q4_v[2 * n], q4_v[2 * n + 1]], e4_v[2 * n : 2 * n + 2])

    def other(index):
        return index + 1 - 2 * (index % 2)

    def coupled(q, matrix):
        return fold(dot(pair(q), matrix))

    def down(g, matrix):
        return fold(dot_nt(pair(g), matrix))

    g = coupled(q5_v[other(group // 4)], cs_v[5])
    g = coupled(q4_v[other(group // 2)], cs_v[4]) + down(g, e4_v[group // 2])
    g = coupled(q3_v[other(group)], cs_v[3]) + down(g, e3_v[group])
    g = coupled(q2_v[other(pos // 4)], cs_v[2]) + down(g, e2_v[pos // 4])
    g = coupled(q1_v[other(pos // 2)], cs_v[1]) + down(g, e1_v[pos // 2])
    g = coupled(q0_v[other(pos)], cs_v[0]) + down(g, e0_v[pos])

    def both_down(q_even, q_odd, coupling, g, e_even, e_odd):
        even = fold(dot(pair(q_odd), coupling)) + down(g, e_even)
        odd = fold(dot_nt(pair(q_even), coupling)) + down(g, e_odd)
        return even, odd

    g_mids = both_down(mids[0], mids[1], cl_v[2], g, tl_v[4], tl_v[5])
    for n in range(2):
        g_leaves = both_down(
            leaves[2 * n], leaves[2 * n + 1], cl_v[n], g_mids[n], tl_v[2 * n], tl_v[2 * n + 1]
        )
        for s in range(2):
            i = 2 * n + s
            at = slice(LEAF * i, LEAF * (i + 1))
            hi, lo = split(g_leaves[s])
            both = jnp.concatenate([hi, lo], axis=0)
            far = fold(dot_nt(both, bhi_v[at, :])) + dot_nt(hi, blo_v[at, :])
            y = OUTPUT_SCALE * (near_v[:, at] + far) + NOISE_VAR * x_v[:, at]
            for b in range(4):
                y_v[4 * i + b] = y[:, 128 * b : 128 * (b + 1)]

    @pl.loop(0, TILES)
    def _(i):
        o = (me // 4 + i) % TILES
        tile = gather_tile(lambda s: y_v[s], inv_v[pl.ds(o, 1), :])
        send_tile(tile, o, b_s, b_r, 4, 2)

    receive_tiles(b_s, b_r, 4, 2)

    @pl.loop(0, TILES)
    def _(o):
        at = pl.ds(pl.multiple_of(o * 128, 128), 128)
        out_v[:, at] = gather_tile(lambda s: xs_v[s], back_v[pl.ds(o, 1), :])


def body(probes, perm, points, anchors, trans_low, couple_low, trans_top, couple_top):
    vmem = pltpu.VMEM
    dma = pltpu.SemaphoreType.DMA
    return pl.pallas_call(
        kernel,
        out_shape=jax.ShapeDtypeStruct((PRB, PTS), F32),
        in_specs=[pl.BlockSpec(memory_space=pl.ANY)] * 8,
        out_specs=pl.BlockSpec(memory_space=pltpu.VMEM),
        scratch_shapes=[
            vmem((TILES, 128), I32),
            vmem((8, PTS), F32),
            vmem((3, L_DEV * R), F32),
            vmem((PRB, PTS), F32),
            vmem((6, R, R), BF16),
            vmem((3, R, R), BF16),
            vmem((8, R, R), BF16),
            vmem((4, R, R), BF16),
            vmem((2, R, R), BF16),
            vmem((8, R, R), BF16),
            vmem((4, R, R), BF16),
            vmem((6, R, R), BF16),
            vmem((6, R, R), BF16),
            vmem((TILES, 128), I32),
            vmem((TILES, 128), I32),
            vmem((TILES, 128), I32),
            vmem((TILES, 128), I32),
            vmem((PTS, 8), F32),
            vmem((PTS, LEAF), BF16),
            vmem((PTS, LEAF), BF16),
            vmem((PTS, R), BF16),
            vmem((PTS, R), BF16),
            vmem((PRB, PTS), F32),
            vmem((2 * PRB, PTS), BF16),
            vmem((TILES, PRB, 128), F32),
            vmem((TILES, PRB, 128), F32),
            vmem((PRB, PTS), F32),
            vmem((N, 1, 128), I32),
            vmem((N, 1, 128), I32),
            vmem((N, 4, 128), F32),
            vmem((N, 4, 128), F32),
            vmem((N, 4, 128), F32),
            vmem((N, 4, 128), F32),
            vmem((8, PRB, R), F32),
            vmem((4, PRB, R), F32),
            vmem((2, PRB, R), F32),
            vmem((8, PRB, R), F32),
            vmem((4, PRB, R), F32),
            vmem((2, PRB, R), F32),
            dma((17,)),
            dma((5,)),
            dma((5,)),
            dma((3,)),
        ],
        compiler_params=pltpu.CompilerParams(
            collective_id=0, has_side_effects=True, vmem_limit_bytes=40 * 1024 * 1024
        ),
        name="hss_product",
    )(perm.reshape(TILES, 128), points, anchors, probes, trans_low, couple_low, trans_top, couple_top)


def solution(mesh):
    placed = (
        P("probe", "leaf"),
        P("leaf"),
        P(None, "leaf"),
        P(None, "leaf"),
        P("leaf", None, None, None),
        P("leaf", None, None, None),
        P(),
        P(),
    )
    return jax.shard_map(
        body, mesh=mesh, in_specs=placed, out_specs=P("probe", "leaf"), check_vma=False
    )
```

time: 185 us -> 68.6 us (0.37)
  matrix products: 65.9 us -> 0 us
  Pallas kernels: 0 us -> 58.9 us
  blocking collectives: 48.9 us -> 0 us
  waiting for transfers between devices: 29.9 us -> 0 us
  starting transfers between devices: 23.4 us -> 0 us
  other arithmetic: 8.47 us -> 0 us
    dot_general x53 -> x0, matrix products: 65.9 us -> none  [the longest x20 38.8 us: match_block(): return jnp.einsum('ps,ts->pt', values, selector, precision=EXACT_MATMUL)]
    pallas_call x0 -> x1, Pallas kernels: none -> 58.9 us  [body(): pl.pallas_call(kernel, out_shape=jax.ShapeDtypeStruct((PRB, PTS), F32), i...]
    all_gather x1 -> x0, blocking collectives: 48.9 us -> none  [body(): gathered = lax.all_gather(summit[None], 'leaf', axis=0, tiled=True)]
    all_to_all x3 -> x0, waiting for transfers between devices: 29.9 us -> none  [the longest x1 10.4 us: body(): lax.all_to_all(picked, 'leaf', split_axis=1, concat_axis=1, tiled=True)]
    all_to_all x3 -> x0, starting transfers between devices: 23.4 us -> none  [the longest x1 13 us: body(): lax.all_to_all(wanted, 'leaf', split_axis=0, concat_axis=0, tiled=True)]
    unnamed x21 -> x17, local copies, waits for them, and re-layouts: 2.19 us -> 9.28 us
    reduce_sum x4 -> x0, other arithmetic: 4.25 us -> none  [rank_block(): return jnp.sum(matches.astype(jnp.int32), axis=1)]
    all_to_all x3 -> x0, other arithmetic: 2.6 us -> none  [the longest x1 0.94 us: body(): lax.all_to_all(outgoing, 'leaf', split_axis=1, concat_axis=1, tiled=True)]
  transfers between devices with their start and end apart: 3 -> 0, of which waited for: 3 -> 0; matrix products, arithmetic and copies ran while one was open for 0% -> 0% of each run, Pallas kernels for 0% -> 0%
where the time goes in v1:
time: 68.6 us; the launch traced here: 68.2 us
  Pallas kernels  58.9 us (86%)
  local copies, waits for them, and re-layouts  9.28 us (14%)
    pallas_call x1, Pallas kernels, body(): pl.pallas_call(kernel, out_shape=jax.ShapeDtypeStruct((PRB, PTS), F32), i...  58.9 us
    unnamed x17, local copies, waits for them, and re-layouts  9.28 us

profile of v1, /device:TPU:1, one launch (start us, length us, event | category | flops | bytes accessed | tf_op | source)
XLA Modules:
  0.0 68.2 jit_solution(2854890798453947348)
XLA Ops:
  0.0 0.0 copy-start
  0.0 2.2 %copy-done = bf16[126,128,128]{2,1,0:T(8,128)(2,1)S(1)} copy-done((bf16[126,128,128]{2,1,0:T(8,128)(2,1)S(1)}, bf16[126,128,128]{2,1,0:T(8,128)(2,1)}, u32[]{:S(2)}) %copy-start) | copy-done | bytes 4128792
  2.2 0.0 copy-start.1
  2.2 1.6 %copy-done.1 = bf16[63,128,128]{2,1,0:T(8,128)(2,1)S(1)} copy-done((bf16[63,128,128]{2,1,0:T(8,128)(2,1)S(1)}, bf16[63,128,128]{2,1,0:T(8,128)(2,1)}, u32[]{:S(2)}) %copy-start.1) | copy-done | bytes 2064408
  3.8 0.0 copy-start.2
  3.8 0.9 %copy-done.2 = bf16[1,6,128,128]{3,2,1,0:T(8,128)(2,1)S(1)} copy-done((bf16[1,6,128,128]{3,2,1,0:T(8,128)(2,1)S(1)}, bf16[1,6,128,128]{3,2,1,0:T(8,128)(2,1)}, u32[]{:S(2)}) %copy-start.2) | copy-done | bytes 196632
  4.7 0.0 copy-start.3
  4.7 0.9 %copy-done.3 = f32[16,2048]{1,0:T(8,128)S(1)} copy-done((f32[16,2048]{1,0:T(8,128)S(1)}, f32[16,2048]{1,0:T(8,128)}, u32[]{:S(2)}) %copy-start.3) | copy-done | bytes 131096
  5.6 0.0 copy-start.4
  5.6 0.9 %copy-done.4 = bf16[1,3,128,128]{3,2,1,0:T(8,128)(2,1)S(1)} copy-done((bf16[1,3,128,128]{3,2,1,0:T(8,128)(2,1)S(1)}, bf16[1,3,128,128]{3,2,1,0:T(8,128)(2,1)}, u32[]{:S(2)}) %copy-start.4) | copy-done | bytes 98328
  6.5 0.0 copy-start.5
  6.5 0.8 %copy-done.5 = f32[3,2048]{1,0:T(4,128)S(1)} copy-done((f32[3,2048]{1,0:T(4,128)S(1)}, f32[3,2048]{1,0:T(4,128)}, u32[]{:S(2)}) %copy-start.5) | copy-done | bytes 24600
  7.2 0.0 copy-start.6
  7.2 0.7 %copy-done.6 = s32[2048]{0:T(1024)S(1)} copy-done((s32[2048]{0:T(1024)S(1)}, s32[2048]{0:T(1024)}, u32[]{:S(2)}) %copy-start.6) | copy-done | bytes 8216
  7.9 0.0 copy-start.7
  7.9 0.7 %copy-done.7 = f32[3,512]{1,0:T(4,128)S(1)} copy-done((f32[3,512]{1,0:T(4,128)S(1)}, f32[3,512]{1,0:T(4,128)}, u32[]{:S(2)}) %copy-start.7) | copy-done | bytes 6168
  8.6 58.9 %hss_product.1 = f32[16,2048]{1,0:T(8,128)S(1)} custom-call(s32[16,128]{1,0:T(8,128)S(1)} %bitcast.1, f32[3,2048]{1,0:T(4,128)S(1)} %copy-done.5, f32[3,512]{1,0:T(4,128)S(1)} %copy-done.7, f32[16,2048]{1,0:T(8,128)S(1)} %copy-done.3, bf16[1,6,128,128]{3,2,1,0:T(8,128)(2,1)S(1)} %copy-done.2, bf16[1,3,128,128]{3,2,1,0:T(8,128)(2,1)S(1)} %copy-done.4, ...), custom_call_target="tpu_custom_call" | custom-call | tf_op jit(solution)/shard_map/hss_product/pallas_call | solution.py:395
  67.5 0.7 copy.10
Async XLA Ops:
  0.0 2.2 %copy-start = (bf16[126,128,128]{2,1,0:T(8,128)(2,1)S(1)}, bf16[126,128,128]{2,1,0:T(8,128)(2,1)}, u32[]{:S(2)}) copy-start(bf16[126,128,128]{2,1,0:T(8,128)(2,1)} %tt_h.1) | copy-start | bytes 12386308
  2.2 1.6 %copy-start.1 = (bf16[63,128,128]{2,1,0:T(8,128)(2,1)S(1)}, bf16[63,128,128]{2,1,0:T(8,128)(2,1)}, u32[]{:S(2)}) copy-start(bf16[63,128,128]{2,1,0:T(8,128)(2,1)} %ct_h.1) | copy-start | bytes 6193156
  3.8 0.9 %copy-start.2 = (bf16[1,6,128,128]{3,2,1,0:T(8,128)(2,1)S(1)}, bf16[1,6,128,128]{3,2,1,0:T(8,128)(2,1)}, u32[]{:S(2)}) copy-start(bf16[1,6,128,128]{3,2,1,0:T(8,128)(2,1)} %tl_h.1) | copy-start | bytes 589828
  4.7 0.9 %copy-start.3 = (f32[16,2048]{1,0:T(8,128)S(1)}, f32[16,2048]{1,0:T(8,128)}, u32[]{:S(2)}) copy-start(f32[16,2048]{1,0:T(8,128)} %probes_h.1) | copy-start | bytes 393220
  5.6 0.9 %copy-start.4 = (bf16[1,3,128,128]{3,2,1,0:T(8,128)(2,1)S(1)}, bf16[1,3,128,128]{3,2,1,0:T(8,128)(2,1)}, u32[]{:S(2)}) copy-start(bf16[1,3,128,128]{3,2,1,0:T(8,128)(2,1)} %cl_h.1) | copy-start | bytes 294916
  6.5 0.8 %copy-start.5 = (f32[3,2048]{1,0:T(4,128)S(1)}, f32[3,2048]{1,0:T(4,128)}, u32[]{:S(2)}) copy-start(f32[3,2048]{1,0:T(4,128)} %points_h.1) | copy-start | bytes 73732
  7.2 0.7 %copy-start.6 = (s32[2048]{0:T(1024)S(1)}, s32[2048]{0:T(1024)}, u32[]{:S(2)}) copy-start(s32[2048]{0:T(1024)} %param.9) | copy-start | bytes 24580
  7.9 0.7 %copy-start.7 = (f32[3,512]{1,0:T(4,128)S(1)}, f32[3,512]{1,0:T(4,128)}, u32[]{:S(2)}) copy-start(f32[3,512]{1,0:T(4,128)} %anchors_h.1) | copy-start | bytes 18436

commit v2 on v1

--- a/solution.py
+++ b/solution.py
@@ -84,6 +84,10 @@
     return jnp.concatenate([out0, out1], axis=0)
 
 
+def near_order(v):
+    return v + (v // 2) * (1 - 2 * (v % 2))
+
+
 def by_lane_block(rows):
     block = iota((1, 128), 1) >> 5
     out = rows[3]
@@ -99,14 +103,19 @@
     e0_v, e1_v, e2_v, e3_v, e4_v, ct_v, cs_v,
     slot_v, inv_v, asked_v, back_v,
     ptst_v, dhi_v, dlo_v, bhi_v, blo_v,
-    x_v, x2_v, xs_v, y_v, near_v,
+    x_v, x2_v, y_v, near_v,
     idx_s, idx_r, a_s, a_r, b_s, b_r,
     q0_v, q1_v, q2_v, q3_v, q4_v, q5_v,
-    load_sem, send_sem, recv_sem, own_sem,
+    load_sem, send_sem, recv_sem, quad_sem,
 ):
     me = lax.axis_index("leaf")
     group = me // 8
     pos = me % 8
+
+    def quad(k):
+        along_z = ((me // 4) % 4 + near_order(k // 4)) % 4
+        along_x = (me // 16 + near_order(k % 4)) % 4
+        return along_x * 4 + along_z
 
     loads = [
         pltpu.make_async_copy(perm_h, perm_v, load_sem.at[0]),
@@ -136,11 +145,36 @@
     def _(k):
         pl.semaphore_signal(barrier, inc=1, device_id={"leaf": (me + k) % N}, device_id_type=MESH)
 
-    def remote(src, dst, which, peer):
+    def remote(src, dst, which, peer, landed=None):
         return pltpu.make_async_remote_copy(
-            src_ref=src, dst_ref=dst, send_sem=send_sem.at[which], recv_sem=recv_sem.at[which],
+            src_ref=src, dst_ref=dst, send_sem=send_sem.at[which],
+            recv_sem=recv_sem.at[which] if landed is None else landed,
             device_id={"leaf": peer}, device_id_type=MESH,
         )
+
+    def send_quad(k, s_ref, r_ref, which):
+        o = quad(k)
+        for h in range(4):
+            peer = 4 * o + h
+
+            def start():
+                remote(s_ref.at[peer], r_ref.at[me], which, peer, quad_sem.at[which, me // 4]).start()
+
+            if isinstance(k, int) and k == 0:
+                pl.when(peer != me)(start)
+            else:
+                start()
+
+    def await_quad(k, s_ref, r_ref, which):
+        count = 3 if isinstance(k, int) and k == 0 else 4
+        o = quad(k)
+        at = pl.ds(0, count)
+        remote(s_ref.at[at], r_ref.at[at], which, me, quad_sem.at[which, o]).wait_recv()
+        return o
+
+    def sent_all(s_ref, r_ref, which):
+        at = pl.ds(0, N - 1)
+        remote(s_ref.at[at], r_ref.at[at], which, me).wait_send()
 
     loads[0].wait()
     row64 = iota((N, 128), 0)
@@ -181,16 +215,6 @@
     for o in range(TILES):
         inv_v[o : o + 1, :] = by_lane_block([places[4 * o + b : 4 * o + b + 1, :] for b in range(4)])
 
-    pl.semaphore_wait(barrier, N - 1)
-
-    @pl.loop(1, N)
-    def _(k):
-        peer = (me + k) % N
-        remote(idx_s.at[peer], idx_r.at[me], 0, peer).start()
-
-    own = pltpu.make_async_copy(idx_s.at[me], idx_r.at[me], own_sem.at[0])
-    own.start()
-
     loads[1].wait()
     loads[2].wait()
     for b in range(TILES):
@@ -212,67 +236,81 @@
         bhi_v[at, :] = hi
         blo_v[at, :] = lo
 
-    own.wait()
-    remote(idx_s.at[pl.ds(0, N - 1)], idx_r.at[pl.ds(0, N - 1)], 0, me).wait()
-
-    for o in range(TILES):
-        asked_v[o : o + 1, :] = by_lane_block([idx_r[4 * o + b] for b in range(4)])
-
+    pl.semaphore_wait(barrier, N - 1)
+
+    @pl.loop(0, TILES - 1)
+    def _(i):
+        send_quad(TILES - 1 - i, idx_s, idx_r, 0)
+
+    send_quad(0, idx_s, idx_r, 0)
+    idx_r[me] = idx_s[me]
+
+    drows = 32
+
+    def dense(leaf):
+        @pl.loop(0, LEAF // drows)
+        def _(i):
+            at = pl.ds(pl.multiple_of(leaf * LEAF + i * drows, drows), drows)
+            total = None
+            for c in range(3):
+                left = ptst_v[at, c : c + 1]
+                right = points_v[c : c + 1, leaf * LEAF : (leaf + 1) * LEAF]
+                differ = left - right
+                total = differ * differ if total is None else total + differ * differ
+            hi, lo = split(jnp.exp(-SHARPNESS * total))
+            dhi_v[at, :] = hi
+            dlo_v[at, :] = lo
+
+    dense(0)
     loads[3].wait()
 
-    def send_tile(tile, o, s_ref, r_ref, which, own_at):
+    def send_tile(tile, k, s_ref, r_ref, which):
+        o = quad(k)
         halves = swap_blocks(tile)
         for h in range(4):
             s_ref[4 * o + h] = halves[h // 2][4 * (h % 2) : 4 * (h % 2) + 4]
-        for h in range(4):
-            peer = 4 * o + h
-
-            @pl.when(peer != me)
-            def _():
-                remote(s_ref.at[peer], r_ref.at[me], which, peer).start()
-
-            @pl.when(peer == me)
-            def _():
-                pltpu.make_async_copy(s_ref.at[peer], r_ref.at[me], own_sem.at[own_at]).start()
-
-    def receive_tiles(s_ref, r_ref, which, own_at):
-        pltpu.make_async_copy(s_ref.at[me], r_ref.at[me], own_sem.at[own_at]).wait()
-        remote(s_ref.at[pl.ds(0, N - 1)], r_ref.at[pl.ds(0, N - 1)], which, me).wait()
-
-        @pl.loop(0, TILES)
-        def _(o):
-            parts = [r_ref[4 * o + h] for h in range(4)]
-            both = jnp.concatenate(parts, axis=0)
-            out = swap_blocks(both)
-            xs_v[o] = jnp.concatenate(out, axis=0)
-
-    @pl.loop(0, TILES)
-    def _(i):
-        o = (me // 4 + i) % TILES
-        tile = gather_tile(lambda s: probes_v[:, 128 * s : 128 * (s + 1)], asked_v[pl.ds(o, 1), :])
-        send_tile(tile, o, a_s, a_r, 1, 1)
-
-    drows = 32
-
-    @pl.loop(0, PTS // drows)
-    def _(i):
-        at = pl.ds(pl.multiple_of(i * drows, drows), drows)
-        leaf = i // (LEAF // drows)
-        total = None
-        for c in range(3):
-            left = ptst_v[at, c : c + 1]
-            right = points_v[c : c + 1, pl.ds(pl.multiple_of(leaf * LEAF, LEAF), LEAF)]
-            differ = left - right
-            total = differ * differ if total is None else total + differ * differ
-        hi, lo = split(jnp.exp(-SHARPNESS * total))
-        dhi_v[at, :] = hi
-        dlo_v[at, :] = lo
+        send_quad(k, s_ref, r_ref, which)
+
+    def take_quads(s_ref, r_ref, which, slots, out):
+        def take(k):
+            o = await_quad(k, s_ref, r_ref, which)
+            source = swap_blocks(jnp.concatenate([r_ref[4 * o + h] for h in range(4)], axis=0))
+            for j in range(TILES):
+                index = jnp.broadcast_to(slots[j : j + 1, :], (8, 128))
+                lane = index & 127
+                here = (index >> 7) == o
+                for v in range(2):
+                    at = (slice(8 * v, 8 * v + 8), slice(128 * j, 128 * (j + 1)))
+                    got = jnp.take_along_axis(source[v], lane, axis=1, mode="promise_in_bounds")
+                    out[at] = jnp.where(here, got, 0.0 if isinstance(k, int) else out[at])
+
+        r_ref[me] = s_ref[me]
+        take(0)
+
+        @pl.loop(1, TILES)
+        def _(k):
+            take(k)
+
+    def pick(k):
+        o = await_quad(k, idx_s, idx_r, 0)
+        asked = by_lane_block([idx_r[4 * o + b] for b in range(4)])
+        asked_v[o] = asked
+        tile = gather_tile(lambda s: probes_v[:, 128 * s : 128 * (s + 1)], asked)
+        send_tile(tile, k, a_s, a_r, 1)
+
+    pick(0)
+
+    @pl.loop(1, TILES)
+    def _(k):
+        pick(k)
+
+    dense(1)
 
     found = jnp.zeros((2 * TILES, 128), F32)
     row16 = iota((TILES, 128), 0)
     row128 = iota((128, 128), 0)
     for o in range(TILES):
-        asked = asked_v[o : o + 1, :]
+        asked = asked_v[o]
         one = (row16 == (asked >> 7)).astype(F32)
         left = jnp.concatenate([one * float(o), one * lane1.astype(F32)], axis=0).astype(BF16)
         right = (row128 == (asked & 127)).astype(F32).astype(BF16)
@@ -286,14 +324,10 @@
         odd = (me // (1 << t)) % 2
         cs_v[t] = jnp.where(odd == 1, jnp.transpose(mat), mat).astype(BF16)
 
-    receive_tiles(a_s, a_r, 1, 1)
-
-    @pl.loop(0, TILES)
-    def _(o):
-        tile = gather_tile(lambda s: xs_v[s], slot_v[pl.ds(o, 1), :])
-        at = pl.ds(pl.multiple_of(o * 128, 128), 128)
-        x_v[:, at] = tile
-        x2_v[:, at] = pair(tile)
+    take_quads(a_s, a_r, 1, slot_v, x_v)
+    for o in range(TILES):
+        at = slice(128 * o, 128 * (o + 1))
+        x2_v[:, at] = pair(x_v[:, at])
 
     def up(children, transfers):
         lhs = pair(jnp.concatenate(children, axis=1))
@@ -310,16 +344,16 @@
     @pl.loop(1, 8)
     def _(k):
         peer = group * 8 + (pos + k) % 8
-        remote(q0_v.at[pos], q0_v.at[pos], 2, peer).start()
+        remote(q0_v.at[pos], q0_v.at[pos], 3, peer).start()
 
     def near(i):
         x2 = x2_v[:, LEAF * i : LEAF * (i + 1)]
         at = slice(LEAF * i, LEAF * (i + 1))
         near_v[:, at] = fold(dot(x2, dhi_v[at, :])) + dot(x2[:PRB], dlo_v[at, :])
 
+    dense(2)
     near(0)
-    near(1)
-    remote(q0_v.at[pl.ds(0, 7)], q0_v.at[pl.ds(0, 7)], 2, me).wait()
+    remote(q0_v.at[pl.ds(0, 7)], q0_v.at[pl.ds(0, 7)], 3, me).wait()
     for n in range(4):
         q1_v[n] = up([q0_v[2 * n], q0_v[2 * n + 1]], e0_v[2 * n : 2 * n + 2])
     for n in range(2):
@@ -329,11 +363,13 @@
     @pl.loop(1, 8)
     def _(k):
         peer = ((group + k) % 8) * 8 + pos
-        remote(q3_v.at[group], q3_v.at[group], 3, peer).start()
-
+        remote(q3_v.at[group], q3_v.at[group], 4, peer).start()
+
+    dense(3)
+    near(1)
     near(2)
     near(3)
-    remote(q3_v.at[pl.ds(0, 7)], q3_v.at[pl.ds(0, 7)], 3, me).wait()
+    remote(q3_v.at[pl.ds(0, 7)], q3_v.at[pl.ds(0, 7)], 4, me).wait()
     for n in range(4):
         q4_v[n] = up([q3_v[2 * n], q3_v[2 * n + 1]], e3_v[2 * n : 2 * n + 2])
     for n in range(2):
@@ -375,18 +411,19 @@
             for b in range(4):
                 y_v[4 * i + b] = y[:, 128 * b : 128 * (b + 1)]
 
-    @pl.loop(0, TILES)
+    def give(k):
+        tile = gather_tile(lambda s: y_v[s], inv_v[pl.ds(quad(k), 1), :])
+        send_tile(tile, k, b_s, b_r, 2)
+
+    @pl.loop(0, TILES - 1)
     def _(i):
-        o = (me // 4 + i) % TILES
-        tile = gather_tile(lambda s: y_v[s], inv_v[pl.ds(o, 1), :])
-        send_tile(tile, o, b_s, b_r, 4, 2)
-
-    receive_tiles(b_s, b_r, 4, 2)
-
-    @pl.loop(0, TILES)
-    def _(o):
-        at = pl.ds(pl.multiple_of(o * 128, 128), 128)
-        out_v[:, at] = gather_tile(lambda s: xs_v[s], back_v[pl.ds(o, 1), :])
+        give(TILES - 1 - i)
+
+    give(0)
+    take_quads(b_s, b_r, 2, back_v, out_v)
+    sent_all(idx_s, idx_r, 0)
+    sent_all(a_s, a_r, 1)
+    sent_all(b_s, b_r, 2)
 
 
 def body(probes, perm, points, anchors, trans_low, couple_low, trans_top, couple_top):
@@ -413,7 +450,7 @@
             vmem((6, R, R), BF16),
             vmem((TILES, 128), I32),
             vmem((TILES, 128), I32),
-            vmem((TILES, 128), I32),
+            vmem((TILES, 1, 128), I32),
             vmem((TILES, 128), I32),
             vmem((PTS, 8), F32),
             vmem((PTS, LEAF), BF16),
@@ -422,7 +459,6 @@
             vmem((PTS, R), BF16),
             vmem((PRB, PTS), F32),
             vmem((2 * PRB, PTS), BF16),
-            vmem((TILES, PRB, 128), F32),
             vmem((TILES, PRB, 128), F32),
             vmem((PRB, PTS), F32),
             vmem((N, 1, 128), I32),
@@ -440,10 +476,10 @@
             dma((17,)),
             dma((5,)),
             dma((5,)),
-            dma((3,)),
+            dma((3, TILES)),
         ],
         compiler_params=pltpu.CompilerParams(
-            collective_id=0, has_side_effects=True, vmem_limit_bytes=40 * 1024 * 1024
+            collective_id=0, has_side_effects=True, vmem_limit_bytes=56 * 1024 * 1024
         ),
         name="hss_product",
     )(perm.reshape(TILES, 128), points, anchors, probes, trans_low, couple_low, trans_top, couple_top)

time: 68.6 us -> 55 us (0.80)
  local copies, waits for them, and re-layouts: 9.28 us -> 1.57 us
  Pallas kernels: 58.9 us -> 53.3 us
    unnamed x17 -> x1, local copies, waits for them, and re-layouts: 9.28 us -> 1.57 us
    pallas_call x1, Pallas kernels: 58.9 us -> 53.3 us  [body(): pl.pallas_call(kernel, out_shape=jax.ShapeDtypeStruct((PRB, PTS), F32), i...]
where the time goes in v2:
time: 55 us; the launch traced here: 54.9 us
  Pallas kernels  53.3 us (97%)
  local copies, waits for them, and re-layouts  1.57 us (3%)
    pallas_call x1, Pallas kernels, body(): pl.pallas_call(kernel, out_shape=jax.ShapeDtypeStruct((PRB, PTS), F32), i...  53.3 us
    unnamed x1, local copies, waits for them, and re-layouts  1.57 us

profile of v2, /device:TPU:1, one launch (start us, length us, event | category | flops | bytes accessed | tf_op | source)
XLA Modules:
  0.0 54.9 jit_solution(18278377891651350468)
XLA Ops:
  0.0 53.3 %hss_product.1 = f32[16,2048]{1,0:T(8,128)} custom-call(s32[16,128]{1,0:T(8,128)} %bitcast.1, f32[3,2048]{1,0:T(4,128)} %points_h.1, f32[3,512]{1,0:T(4,128)} %anchors_h.1, f32[16,2048]{1,0:T(8,128)} %probes_h.1, bf16[1,6,128,128]{3,2,1,0:T(8,128)(2,1)} %tl_h.1, bf16[1,3,128,128]{3,2,1,0:T(8,128)(2,1)} %cl_h.1, bf16[126,128,128]{2,1,0:T(8,128)(2,1)} %tt_h.1, ...), custom_call_target="tpu_custom_call" | custom-call | tf_op jit(solution)/shard_map/hss_product/pallas_call | solution.py:432
  53.3 1.6 %copy.10 = f32[16,2048]{1,0:T(8,128)} copy(f32[16,2048]{1,0:T(8,128)} %hss_product.1) | data formatting | bytes 262144

commit v3 on v2

--- a/solution.py
+++ b/solution.py
@@ -18,6 +18,9 @@
 SHARPNESS = 2.0
 OUTPUT_SCALE = 0.25
 NOISE_VAR = 0.5
+BATCHES = ((0, 8), (8, 16))
+JB = 4
+SB = 8
 MESH = pl.DeviceIdType.MESH
 F32 = jnp.float32
 BF16 = jnp.bfloat16
@@ -103,7 +106,7 @@
     e0_v, e1_v, e2_v, e3_v, e4_v, ct_v, cs_v,
     slot_v, inv_v, asked_v, back_v,
     ptst_v, dhi_v, dlo_v, bhi_v, blo_v,
-    x_v, x2_v, y_v, near_v,
+    x_v, x2_v, xs_v, y_v, near_v,
     idx_s, idx_r, a_s, a_r, b_s, b_r,
     q0_v, q1_v, q2_v, q3_v, q4_v, q5_v,
     load_sem, send_sem, recv_sem, quad_sem,
@@ -195,7 +198,7 @@
         rank = jnp.sum(one * (counts[N * b : N * (b + 1), :128] + base), axis=0, keepdims=True)
         base = base + counts[N * b : N * (b + 1), 128:]
         rank = rank.astype(I32)
-        slot_v[b : b + 1, :] = (entry >> 11) * BLK + rank
+        slot_v[b] = (entry >> 11) * BLK + rank
         offset = entry & (PTS - 1)
         left = jnp.concatenate(
             [
@@ -213,7 +216,7 @@
     for h in range(N):
         idx_s[h] = wanted[h : h + 1, :]
     for o in range(TILES):
-        inv_v[o : o + 1, :] = by_lane_block([places[4 * o + b : 4 * o + b + 1, :] for b in range(4)])
+        inv_v[o] = by_lane_block([places[4 * o + b : 4 * o + b + 1, :] for b in range(4)])
 
     loads[1].wait()
     loads[2].wait()
@@ -264,45 +267,56 @@
     dense(0)
     loads[3].wait()
 
-    def send_tile(tile, k, s_ref, r_ref, which):
-        o = quad(k)
-        halves = swap_blocks(tile)
-        for h in range(4):
-            s_ref[4 * o + h] = halves[h // 2][4 * (h % 2) : 4 * (h % 2) + 4]
-        send_quad(k, s_ref, r_ref, which)
+    def send_tiles(tiles, ks, s_ref, r_ref, which):
+        for tile, k in zip(tiles, ks):
+            o = quad(k)
+            halves = swap_blocks(tile)
+            for h in range(4):
+                s_ref[4 * o + h] = halves[h // 2][4 * (h % 2) : 4 * (h % 2) + 4]
+        for k in ks:
+            send_quad(k, s_ref, r_ref, which)
 
     def take_quads(s_ref, r_ref, which, slots, out):
-        def take(k):
-            o = await_quad(k, s_ref, r_ref, which)
-            source = swap_blocks(jnp.concatenate([r_ref[4 * o + h] for h in range(4)], axis=0))
-            for j in range(TILES):
-                index = jnp.broadcast_to(slots[j : j + 1, :], (8, 128))
-                lane = index & 127
-                here = (index >> 7) == o
-                for v in range(2):
-                    at = (slice(8 * v, 8 * v + 8), slice(128 * j, 128 * (j + 1)))
-                    got = jnp.take_along_axis(source[v], lane, axis=1, mode="promise_in_bounds")
-                    out[at] = jnp.where(here, got, 0.0 if isinstance(k, int) else out[at])
-
         r_ref[me] = s_ref[me]
-        take(0)
-
-        @pl.loop(1, TILES)
-        def _(k):
-            take(k)
-
-    def pick(k):
-        o = await_quad(k, idx_s, idx_r, 0)
-        asked = by_lane_block([idx_r[4 * o + b] for b in range(4)])
-        asked_v[o] = asked
-        tile = gather_tile(lambda s: probes_v[:, 128 * s : 128 * (s + 1)], asked)
-        send_tile(tile, k, a_s, a_r, 1)
-
-    pick(0)
-
-    @pl.loop(1, TILES)
-    def _(k):
-        pick(k)
+        for first, last in BATCHES:
+            ks = range(first, last)
+            homes = [await_quad(k, s_ref, r_ref, which) for k in ks]
+            for k, o in zip(ks, homes):
+                both = swap_blocks(jnp.concatenate([r_ref[4 * o + h] for h in range(4)], axis=0))
+                xs_v[k] = jnp.concatenate(both, axis=0)
+
+            @pl.loop(0, TILES // JB)
+            def _(i):
+                for u in range(JB):
+                    j = i * JB + u
+                    index = jnp.broadcast_to(slots[j], (8, 128))
+                    lane = index & 127
+                    tile = index >> 7
+                    got = [out[j, 8 * v : 8 * v + 8] if first else jnp.zeros((8, 128), F32) for v in range(2)]
+                    for k, o in zip(ks, homes):
+                        here = tile == o
+                        for v in range(2):
+                            part = jnp.take_along_axis(
+                                xs_v[k, 8 * v : 8 * v + 8], lane, axis=1, mode="promise_in_bounds"
+                            )
+                            got[v] = jnp.where(here, part, got[v])
+                    for v in range(2):
+                        out[j, 8 * v : 8 * v + 8] = got[v]
+
+    def pick(ks):
+        tiles = []
+        for k in ks:
+            o = await_quad(k, idx_s, idx_r, 0)
+            asked = by_lane_block([idx_r[4 * o + b] for b in range(4)])
+            asked_v[o] = asked
+            tiles.append(gather_tile(lambda s: probes_v[:, 128 * s : 128 * (s + 1)], asked))
+        send_tiles(tiles, ks, a_s, a_r, 1)
+
+    pick(list(range(SB)))
+
+    @pl.loop(1, TILES // SB)
+    def _(i):
+        pick([SB * i + u for u in range(SB)])
 
     dense(1)
 
@@ -315,7 +329,9 @@
         left = jnp.concatenate([one * float(o), one * lane1.astype(F32)], axis=0).astype(BF16)
         right = (row128 == (asked & 127)).astype(F32).astype(BF16)
         found = found + dot_nt(left, right)
-    back_v[...] = (found[:TILES] * 128.0 + found[TILES:]).astype(I32)
+    back = (found[:TILES] * 128.0 + found[TILES:]).astype(I32)
+    for o in range(TILES):
+        back_v[o] = back[o : o + 1, :]
 
     for copy in loads[4:]:
         copy.wait()
@@ -326,8 +342,7 @@
 
     take_quads(a_s, a_r, 1, slot_v, x_v)
     for o in range(TILES):
-        at = slice(128 * o, 128 * (o + 1))
-        x2_v[:, at] = pair(x_v[:, at])
+        x2_v[:, 128 * o : 128 * (o + 1)] = pair(x_v[o])
 
     def up(children, transfers):
         lhs = pair(jnp.concatenate(children, axis=1))
@@ -407,20 +422,22 @@
             hi, lo = split(g_leaves[s])
             both = jnp.concatenate([hi, lo], axis=0)
             far = fold(dot_nt(both, bhi_v[at, :])) + dot_nt(hi, blo_v[at, :])
-            y = OUTPUT_SCALE * (near_v[:, at] + far) + NOISE_VAR * x_v[:, at]
+            y = OUTPUT_SCALE * (near_v[:, at] + far)
             for b in range(4):
-                y_v[4 * i + b] = y[:, 128 * b : 128 * (b + 1)]
-
-    def give(k):
-        tile = gather_tile(lambda s: y_v[s], inv_v[pl.ds(quad(k), 1), :])
-        send_tile(tile, k, b_s, b_r, 2)
-
-    @pl.loop(0, TILES - 1)
+                y_v[4 * i + b] = y[:, 128 * b : 128 * (b + 1)] + NOISE_VAR * x_v[4 * i + b]
+
+    def give(ks):
+        tiles = [gather_tile(lambda s: y_v[s], inv_v[quad(k)]) for k in ks]
+        send_tiles(tiles, ks, b_s, b_r, 2)
+
+    @pl.loop(0, TILES // SB - 1)
     def _(i):
-        give(TILES - 1 - i)
-
-    give(0)
-    take_quads(b_s, b_r, 2, back_v, out_v)
+        give([TILES - 1 - SB * i - u for u in range(SB)])
+
+    give(list(range(SB)))
+    take_quads(b_s, b_r, 2, back_v, y_v)
+    for j in range(TILES):
+        out_v[:, 128 * j : 128 * (j + 1)] = y_v[j]
     sent_all(idx_s, idx_r, 0)
     sent_all(a_s, a_r, 1)
     sent_all(b_s, b_r, 2)
@@ -448,17 +465,18 @@
             vmem((4, R, R), BF16),
             vmem((6, R, R), BF16),
             vmem((6, R, R), BF16),
-            vmem((TILES, 128), I32),
-            vmem((TILES, 128), I32),
             vmem((TILES, 1, 128), I32),
-            vmem((TILES, 128), I32),
+            vmem((TILES, 1, 128), I32),
+            vmem((TILES, 1, 128), I32),
+            vmem((TILES, 1, 128), I32),
             vmem((PTS, 8), F32),
             vmem((PTS, LEAF), BF16),
             vmem((PTS, LEAF), BF16),
             vmem((PTS, R), BF16),
             vmem((PTS, R), BF16),
-            vmem((PRB, PTS), F32),
+            vmem((TILES, PRB, 128), F32),
             vmem((2 * PRB, PTS), BF16),
+            vmem((TILES, PRB, 128), F32),
             vmem((TILES, PRB, 128), F32),
             vmem((PRB, PTS), F32),
             vmem((N, 1, 128), I32),

time: 55 us -> 49.2 us (0.89)
  Pallas kernels: 53.3 us -> 47.5 us
    pallas_call x1, Pallas kernels: 53.3 us -> 47.5 us  [body(): pl.pallas_call(kernel, out_shape=jax.ShapeDtypeStruct((PRB, PTS), F32), i...]
where the time goes in v3:
time: 49.2 us; the launch traced here: 49.1 us
  Pallas kernels  47.5 us (97%)
  local copies, waits for them, and re-layouts  1.57 us (3%)
    pallas_call x1, Pallas kernels, body(): pl.pallas_call(kernel, out_shape=jax.ShapeDtypeStruct((PRB, PTS), F32), i...  47.5 us
    unnamed x1, local copies, waits for them, and re-layouts  1.57 us

profile of v3, /device:TPU:1, one launch (start us, length us, event | category | flops | bytes accessed | tf_op | source)
XLA Modules:
  0.0 49.1 jit_solution(9732819020684095768)
XLA Ops:
  0.0 47.5 %hss_product.1 = f32[16,2048]{1,0:T(8,128)} custom-call(s32[16,128]{1,0:T(8,128)} %bitcast.1, f32[3,2048]{1,0:T(4,128)} %points_h.1, f32[3,512]{1,0:T(4,128)} %anchors_h.1, f32[16,2048]{1,0:T(8,128)} %probes_h.1, bf16[1,6,128,128]{3,2,1,0:T(8,128)(2,1)} %tl_h.1, bf16[1,3,128,128]{3,2,1,0:T(8,128)(2,1)} %cl_h.1, bf16[126,128,128]{2,1,0:T(8,128)(2,1)} %tt_h.1, ...), custom_call_target="tpu_custom_call" | custom-call | tf_op jit(solution)/shard_map/hss_product/pallas_call | solution.py:449
  47.5 1.6 %copy.10 = f32[16,2048]{1,0:T(8,128)} copy(f32[16,2048]{1,0:T(8,128)} %hss_product.1) | data formatting | bytes 262144

commit v4 on v3

--- a/solution.py
+++ b/solution.py
@@ -16,11 +16,13 @@
 BLK = PTS // N
 TILES = PTS // 128
 SHARPNESS = 2.0
+LOG2_E = 1.4426950408889634
 OUTPUT_SCALE = 0.25
 NOISE_VAR = 0.5
 BATCHES = ((0, 8), (8, 16))
 JB = 4
 SB = 8
+PB = 4
 MESH = pl.DeviceIdType.MESH
 F32 = jnp.float32
 BF16 = jnp.bfloat16
@@ -48,6 +50,23 @@
 
 def fold(r):
     return r[:PRB] + r[PRB:]
+
+
+def fold_lanes(r):
+    return r[:, :R] + r[:, R:]
+
+
+def times_exact(pieces, matrix):
+    r = dot(jnp.concatenate(pieces, axis=0), matrix)
+    return split(r[:R] + r[R:])
+
+
+def exact_times(matrix, pieces):
+    return split(fold_lanes(dot(matrix, jnp.concatenate(pieces, axis=1))))
+
+
+def exact_times_turned(matrix, pieces):
+    return split(fold_lanes(dot_nt(matrix, jnp.concatenate(pieces, axis=0))))
 
 
 def iota(shape, dim):
@@ -105,10 +124,10 @@
     perm_v, points_v, anchors_v, probes_v, tl_v, cl_v,
     e0_v, e1_v, e2_v, e3_v, e4_v, ct_v, cs_v,
     slot_v, inv_v, asked_v, back_v,
-    ptst_v, dhi_v, dlo_v, bhi_v, blo_v,
-    x_v, x2_v, xs_v, y_v, near_v,
+    ptst_v, dhi_v, dlo_v, bhi_v, blo_v, uhi_v, ulo_v, f1_v, whi_v, wlo_v,
+    x_v, x2_v, xs_v, y_v,
     idx_s, idx_r, a_s, a_r, b_s, b_r,
-    q0_v, q1_v, q2_v, q3_v, q4_v, q5_v,
+    q0_v, q1_v, q2_v, q3_v, q4_v,
     load_sem, send_sem, recv_sem, quad_sem,
 ):
     me = lax.axis_index("leaf")
@@ -218,6 +237,15 @@
     for o in range(TILES):
         inv_v[o] = by_lane_block([places[4 * o + b : 4 * o + b + 1, :] for b in range(4)])
 
+    pl.semaphore_wait(barrier, N - 1)
+
+    @pl.loop(0, TILES - 1)
+    def _(i):
+        send_quad(TILES - 1 - i, idx_s, idx_r, 0)
+
+    send_quad(0, idx_s, idx_r, 0)
+    idx_r[me] = idx_s[me]
+
     loads[1].wait()
     loads[2].wait()
     for b in range(TILES):
@@ -235,18 +263,9 @@
             right = anchors_v[c : c + 1, pl.ds(pl.multiple_of(leaf * R, R), R)]
             differ = left - right
             total = differ * differ if total is None else total + differ * differ
-        hi, lo = split(jnp.exp(-SHARPNESS * total))
+        hi, lo = split(jnp.exp2((-SHARPNESS * LOG2_E) * total))
         bhi_v[at, :] = hi
         blo_v[at, :] = lo
-
-    pl.semaphore_wait(barrier, N - 1)
-
-    @pl.loop(0, TILES - 1)
-    def _(i):
-        send_quad(TILES - 1 - i, idx_s, idx_r, 0)
-
-    send_quad(0, idx_s, idx_r, 0)
-    idx_r[me] = idx_s[me]
 
     drows = 32
 
@@ -260,11 +279,10 @@
                 right = points_v[c : c + 1, leaf * LEAF : (leaf + 1) * LEAF]
                 differ = left - right
                 total = differ * differ if total is None else total + differ * differ
-            hi, lo = split(jnp.exp(-SHARPNESS * total))
+            hi, lo = split(jnp.exp2((-SHARPNESS * LOG2_E) * total))
             dhi_v[at, :] = hi
             dlo_v[at, :] = lo
 
-    dense(0)
     loads[3].wait()
 
     def send_tiles(tiles, ks, s_ref, r_ref, which):
@@ -312,13 +330,12 @@
             tiles.append(gather_tile(lambda s: probes_v[:, 128 * s : 128 * (s + 1)], asked))
         send_tiles(tiles, ks, a_s, a_r, 1)
 
-    pick(list(range(SB)))
-
-    @pl.loop(1, TILES // SB)
+    pick(list(range(PB)))
+
+    @pl.loop(1, TILES // PB)
     def _(i):
-        pick([SB * i + u for u in range(SB)])
-
-    dense(1)
+        pick([PB * i + u for u in range(PB)])
+
 
     found = jnp.zeros((2 * TILES, 128), F32)
     row16 = iota((TILES, 128), 0)
@@ -333,13 +350,40 @@
     for o in range(TILES):
         back_v[o] = back[o : o + 1, :]
 
-    for copy in loads[4:]:
+    for copy in loads[5:]:
         copy.wait()
     for t in range(6):
         mat = ct_v[t].astype(F32)
         odd = (me // (1 << t)) % 2
         cs_v[t] = jnp.where(odd == 1, jnp.transpose(mat), mat).astype(BF16)
 
+    def other(index):
+        return index + 1 - 2 * (index % 2)
+
+    far_half = other(group // 4)
+    path = split(dot(e0_v[pos], e1_v[pos // 2]))
+    f1_v[0], f1_v[1] = path
+    path = times_exact(path, e2_v[pos // 4])
+    links = [exact_times_turned(cs_v[3], path)]
+    path = times_exact(path, e3_v[group])
+    links.append(exact_times_turned(cs_v[4], path))
+    path = times_exact(path, e4_v[group // 2])
+    last = exact_times_turned(cs_v[5], path)
+    for n in range(2):
+        links.append(exact_times(e4_v[2 * far_half + n], last))
+    for n in range(4):
+        whi_v[R * n : R * (n + 1), :] = links[n][0]
+        wlo_v[R * n : R * (n + 1), :] = links[n][1]
+    loads[4].wait()
+    for i in range(L_DEV):
+        at = slice(LEAF * i, LEAF * (i + 1))
+        hi, lo = split(dot(tl_v[i], tl_v[4 + i // 2]))
+        both = fold_lanes(dot(bhi_v[at, :], jnp.concatenate([hi, lo], axis=1)))
+        hi, lo = split(both + dot(blo_v[at, :], hi))
+        uhi_v[at, :] = hi
+        ulo_v[at, :] = lo
+
+
     take_quads(a_s, a_r, 1, slot_v, x_v)
     for o in range(TILES):
         x2_v[:, 128 * o : 128 * (o + 1)] = pair(x_v[o])
@@ -347,6 +391,33 @@
     def up(children, transfers):
         lhs = pair(jnp.concatenate(children, axis=1))
         return fold(dot(lhs, transfers.reshape(2 * R, R)))
+
+    x2 = x2_v[...]
+    q0_v[pos] = fold(dot(x2, uhi_v[...])) + dot(x2[:PRB], ulo_v[...])
+
+    @pl.loop(1, 8)
+    def _(k):
+        peer = group * 8 + (pos + k) % 8
+        remote(q0_v.at[pos], q0_v.at[pos], 3, peer).start()
+
+    def near(i):
+        x2 = x2_v[:, LEAF * i : LEAF * (i + 1)]
+        at = slice(LEAF * i, LEAF * (i + 1))
+        hi, lo = split(within[i])
+        both = jnp.concatenate([hi, lo], axis=0)
+        inner = fold(dot(x2, dhi_v[at, :])) + dot(x2[:PRB], dlo_v[at, :])
+        inner = inner + fold(dot_nt(both, bhi_v[at, :])) + dot_nt(hi, blo_v[at, :])
+        for b in range(4):
+            y_v[4 * i + b] = OUTPUT_SCALE * inner[:, 128 * b : 128 * (b + 1)] + NOISE_VAR * x_v[4 * i + b]
+
+    dense(0)
+    dense(1)
+
+    def coupled(q, matrix):
+        return fold(dot(pair(q), matrix))
+
+    def down(g, matrix):
+        return fold(dot_nt(pair(g), matrix))
 
     leaves = []
     for i in range(L_DEV):
@@ -354,20 +425,12 @@
         at = slice(LEAF * i, LEAF * (i + 1))
         leaves.append(fold(dot(x2, bhi_v[at, :])) + dot(x2[:PRB], blo_v[at, :]))
     mids = [up(leaves[2 * n : 2 * n + 2], tl_v[2 * n : 2 * n + 2]) for n in range(2)]
-    q0_v[pos] = up(mids, tl_v[4:6])
-
-    @pl.loop(1, 8)
-    def _(k):
-        peer = group * 8 + (pos + k) % 8
-        remote(q0_v.at[pos], q0_v.at[pos], 3, peer).start()
-
-    def near(i):
-        x2 = x2_v[:, LEAF * i : LEAF * (i + 1)]
-        at = slice(LEAF * i, LEAF * (i + 1))
-        near_v[:, at] = fold(dot(x2, dhi_v[at, :])) + dot(x2[:PRB], dlo_v[at, :])
-
-    dense(2)
-    near(0)
+    within_mids = [coupled(mids[1], cl_v[2]), down(mids[0], cl_v[2])]
+    within = []
+    for n in range(2):
+        within.append(coupled(leaves[2 * n + 1], cl_v[n]) + down(within_mids[n], tl_v[2 * n]))
+        within.append(down(leaves[2 * n], cl_v[n]) + down(within_mids[n], tl_v[2 * n + 1]))
+
     remote(q0_v.at[pl.ds(0, 7)], q0_v.at[pl.ds(0, 7)], 3, me).wait()
     for n in range(4):
         q1_v[n] = up([q0_v[2 * n], q0_v[2 * n + 1]], e0_v[2 * n : 2 * n + 2])
@@ -380,51 +443,26 @@
         peer = ((group + k) % 8) * 8 + pos
         remote(q3_v.at[group], q3_v.at[group], 4, peer).start()
 
-    dense(3)
+    part = coupled(q0_v[other(pos)], cs_v[0]) + down(coupled(q1_v[other(pos // 2)], cs_v[1]), e0_v[pos])
+    hi, lo = split(coupled(q2_v[other(pos // 4)], cs_v[2]))
+    both = jnp.concatenate([hi, lo], axis=0)
+    part = part + fold(dot_nt(both, f1_v[0])) + dot_nt(hi, f1_v[1])
+    dense(2)
+    near(0)
     near(1)
     near(2)
+    dense(3)
     near(3)
     remote(q3_v.at[pl.ds(0, 7)], q3_v.at[pl.ds(0, 7)], 4, me).wait()
     for n in range(4):
         q4_v[n] = up([q3_v[2 * n], q3_v[2 * n + 1]], e3_v[2 * n : 2 * n + 2])
-    for n in range(2):
-        q5_v[n] = up([q4_v[2 * n], q4_v[2 * n + 1]], e4_v[2 * n : 2 * n + 2])
-
-    def other(index):
-        return index + 1 - 2 * (index % 2)
-
-    def coupled(q, matrix):
-        return fold(dot(pair(q), matrix))
-
-    def down(g, matrix):
-        return fold(dot_nt(pair(g), matrix))
-
-    g = coupled(q5_v[other(group // 4)], cs_v[5])
-    g = coupled(q4_v[other(group // 2)], cs_v[4]) + down(g, e4_v[group // 2])
-    g = coupled(q3_v[other(group)], cs_v[3]) + down(g, e3_v[group])
-    g = coupled(q2_v[other(pos // 4)], cs_v[2]) + down(g, e2_v[pos // 4])
-    g = coupled(q1_v[other(pos // 2)], cs_v[1]) + down(g, e1_v[pos // 2])
-    g = coupled(q0_v[other(pos)], cs_v[0]) + down(g, e0_v[pos])
-
-    def both_down(q_even, q_odd, coupling, g, e_even, e_odd):
-        even = fold(dot(pair(q_odd), coupling)) + down(g, e_even)
-        odd = fold(dot_nt(pair(q_even), coupling)) + down(g, e_odd)
-        return even, odd
-
-    g_mids = both_down(mids[0], mids[1], cl_v[2], g, tl_v[4], tl_v[5])
-    for n in range(2):
-        g_leaves = both_down(
-            leaves[2 * n], leaves[2 * n + 1], cl_v[n], g_mids[n], tl_v[2 * n], tl_v[2 * n + 1]
-        )
-        for s in range(2):
-            i = 2 * n + s
-            at = slice(LEAF * i, LEAF * (i + 1))
-            hi, lo = split(g_leaves[s])
-            both = jnp.concatenate([hi, lo], axis=0)
-            far = fold(dot_nt(both, bhi_v[at, :])) + dot_nt(hi, blo_v[at, :])
-            y = OUTPUT_SCALE * (near_v[:, at] + far)
-            for b in range(4):
-                y_v[4 * i + b] = y[:, 128 * b : 128 * (b + 1)] + NOISE_VAR * x_v[4 * i + b]
+    tops = [q3_v[other(group)], q4_v[other(group // 2)], q4_v[2 * far_half], q4_v[2 * far_half + 1]]
+    hi, lo = split(jnp.concatenate(tops, axis=1))
+    g = part + fold(dot(jnp.concatenate([hi, lo], axis=0), whi_v[...])) + dot(hi, wlo_v[...])
+    hi, lo = split(g)
+    far = fold(dot_nt(jnp.concatenate([hi, lo], axis=0), uhi_v[...])) + dot_nt(hi, ulo_v[...])
+    for j in range(TILES):
+        y_v[j] = y_v[j] + OUTPUT_SCALE * far[:, 128 * j : 128 * (j + 1)]
 
     def give(ks):
         tiles = [gather_tile(lambda s: y_v[s], inv_v[quad(k)]) for k in ks]
@@ -448,7 +486,7 @@
     dma = pltpu.SemaphoreType.DMA
     return pl.pallas_call(
         kernel,
-        out_shape=jax.ShapeDtypeStruct((PRB, PTS), F32),
+        out_shape=pltpu.VMEM((PRB, PTS), F32),
         in_specs=[pl.BlockSpec(memory_space=pl.ANY)] * 8,
         out_specs=pl.BlockSpec(memory_space=pltpu.VMEM),
         scratch_shapes=[
@@ -474,11 +512,15 @@
             vmem((PTS, LEAF), BF16),
             vmem((PTS, R), BF16),
             vmem((PTS, R), BF16),
+            vmem((PTS, R), BF16),
+            vmem((PTS, R), BF16),
+            vmem((2, R, R), BF16),
+            vmem((4 * R, R), BF16),
+            vmem((4 * R, R), BF16),
             vmem((TILES, PRB, 128), F32),
             vmem((2 * PRB, PTS), BF16),
             vmem((TILES, PRB, 128), F32),
             vmem((TILES, PRB, 128), F32),
-            vmem((PRB, PTS), F32),
             vmem((N, 1, 128), I32),
             vmem((N, 1, 128), I32),
             vmem((N, 4, 128), F32),
@@ -490,7 +532,6 @@
             vmem((2, PRB, R), F32),
             vmem((8, PRB, R), F32),
             vmem((4, PRB, R), F32),
-            vmem((2, PRB, R), F32),
             dma((17,)),
             dma((5,)),
             dma((5,)),

time: 49.2 us -> 46.5 us (0.945)
  Pallas kernels: 47.5 us -> 45.7 us
  local copies, waits for them, and re-layouts: 1.57 us -> 0.66 us
    pallas_call x1, Pallas kernels: 47.5 us -> 45.7 us  [body(): pl.pallas_call(kernel, out_shape=pltpu.VMEM((PRB, PTS), F32), in_specs=[p...]
    unnamed x1, local copies, waits for them, and re-layouts: 1.57 us -> 0.66 us
where the time goes in v4:
time: 46.5 us; the launch traced here: 46.4 us
  Pallas kernels  45.7 us (98%)
  local copies, waits for them, and re-layouts  0.66 us (1%)
    pallas_call x1, Pallas kernels, body(): pl.pallas_call(kernel, out_shape=pltpu.VMEM((PRB, PTS), F32), in_specs=[p...  45.7 us

profile of v4, /device:TPU:1, one launch (start us, length us, event | category | flops | bytes accessed | tf_op | source)
XLA Modules:
  0.0 46.4 jit_solution(7070616551942097329)
XLA Ops:
  0.0 45.7 %hss_product.1 = f32[16,2048]{1,0:T(8,128)S(1)} custom-call(s32[16,128]{1,0:T(8,128)} %bitcast.1, f32[3,2048]{1,0:T(4,128)} %points_h.1, f32[3,512]{1,0:T(4,128)} %anchors_h.1, f32[16,2048]{1,0:T(8,128)} %probes_h.1, bf16[1,6,128,128]{3,2,1,0:T(8,128)(2,1)} %tl_h.1, bf16[1,3,128,128]{3,2,1,0:T(8,128)(2,1)} %cl_h.1, bf16[126,128,128]{2,1,0:T(8,128)(2,1)} %tt_h.1, ...), custom_call_target="tpu_custom_call" | custom-call | tf_op jit(solution)/shard_map/hss_product/pallas_call | solution.py:487
  45.8 0.7 %copy.10 = f32[16,2048]{1,0:T(8,128)} copy(f32[16,2048]{1,0:T(8,128)S(1)} %hss_product.1) | data formatting | bytes 262144

commit v5 on v4

--- a/solution.py
+++ b/solution.py
@@ -22,7 +22,7 @@
 BATCHES = ((0, 8), (8, 16))
 JB = 4
 SB = 8
-PB = 4
+PB = 8
 MESH = pl.DeviceIdType.MESH
 F32 = jnp.float32
 BF16 = jnp.bfloat16
@@ -251,7 +251,7 @@
     for b in range(TILES):
         ptst_v[128 * b : 128 * (b + 1), :] = jnp.transpose(points_v[:, 128 * b : 128 * (b + 1)])
 
-    rows = 64
+    rows = 256
 
     @pl.loop(0, PTS // rows)
     def _(i):
@@ -267,7 +267,7 @@
         bhi_v[at, :] = hi
         blo_v[at, :] = lo
 
-    drows = 32
+    drows = 128
 
     def dense(leaf):
         @pl.loop(0, LEAF // drows)

time: 46.5 us -> 45.4 us (0.976)
  Pallas kernels: 45.7 us -> 44.7 us
    pallas_call x1, Pallas kernels: 45.7 us -> 44.7 us  [body(): pl.pallas_call(kernel, out_shape=pltpu.VMEM((PRB, PTS), F32), in_specs=[p...]
where the time goes in v5:
time: 45.4 us; the launch traced here: 45.3 us
  Pallas kernels  44.7 us (98%)
  local copies, waits for them, and re-layouts  0.66 us (1%)
    pallas_call x1, Pallas kernels, body(): pl.pallas_call(kernel, out_shape=pltpu.VMEM((PRB, PTS), F32), in_specs=[p...  44.7 us

profile of v5, /device:TPU:1, one launch (start us, length us, event | category | flops | bytes accessed | tf_op | source)
XLA Modules:
  0.0 45.3 jit_solution(15600966349048897042)
XLA Ops:
  0.0 44.7 %hss_product.1 = f32[16,2048]{1,0:T(8,128)S(1)} custom-call(s32[16,128]{1,0:T(8,128)} %bitcast.1, f32[3,2048]{1,0:T(4,128)} %points_h.1, f32[3,512]{1,0:T(4,128)} %anchors_h.1, f32[16,2048]{1,0:T(8,128)} %probes_h.1, bf16[1,6,128,128]{3,2,1,0:T(8,128)(2,1)} %tl_h.1, bf16[1,3,128,128]{3,2,1,0:T(8,128)(2,1)} %cl_h.1, bf16[126,128,128]{2,1,0:T(8,128)(2,1)} %tt_h.1, ...), custom_call_target="tpu_custom_call" | custom-call | tf_op jit(solution)/shard_map/hss_product/pallas_call | solution.py:487
  44.7 0.7 %copy.10 = f32[16,2048]{1,0:T(8,128)} copy(f32[16,2048]{1,0:T(8,128)S(1)} %hss_product.1) | data formatting | bytes 262144

commit v6 on v5

--- a/solution.py
+++ b/solution.py
@@ -163,9 +163,18 @@
 
     barrier = pltpu.get_barrier_semaphore()
 
-    @pl.loop(1, N)
-    def _(k):
-        pl.semaphore_signal(barrier, inc=1, device_id={"leaf": (me + k) % N}, device_id_type=MESH)
+    def greet(peer):
+        pl.semaphore_signal(barrier, inc=1, device_id={"leaf": peer}, device_id_type=MESH)
+
+    @pl.loop(0, TILES - 1)
+    def _(i):
+        for h in range(4):
+            greet(4 * quad(TILES - 1 - i) + h)
+
+    for h in range(4):
+        peer = 4 * quad(0) + h
+        pl.when(peer != me)(functools.partial(greet, peer))
+
 
     def remote(src, dst, which, peer, landed=None):
         return pltpu.make_async_remote_copy(
@@ -411,7 +420,6 @@
             y_v[4 * i + b] = OUTPUT_SCALE * inner[:, 128 * b : 128 * (b + 1)] + NOISE_VAR * x_v[4 * i + b]
 
     dense(0)
-    dense(1)
 
     def coupled(q, matrix):
         return fold(dot(pair(q), matrix))
@@ -447,6 +455,7 @@
     hi, lo = split(coupled(q2_v[other(pos // 4)], cs_v[2]))
     both = jnp.concatenate([hi, lo], axis=0)
     part = part + fold(dot_nt(both, f1_v[0])) + dot_nt(hi, f1_v[1])
+    dense(1)
     dense(2)
     near(0)
     near(1)

time: 45.4 us -> 45.1 us (level)
  no operation moved by 1% of the time
where the time goes in v6:
time: 45.1 us; the launch traced here: 45 us
  Pallas kernels  44.4 us (98%)
  local copies, waits for them, and re-layouts  0.66 us (1%)
    pallas_call x1, Pallas kernels, body(): pl.pallas_call(kernel, out_shape=pltpu.VMEM((PRB, PTS), F32), in_specs=[p...  44.4 us

profile of v6, /device:TPU:1, one launch (start us, length us, event | category | flops | bytes accessed | tf_op | source)
XLA Modules:
  0.0 45.0 jit_solution(14538261854539932101)
XLA Ops:
  0.0 44.4 %hss_product.1 = f32[16,2048]{1,0:T(8,128)S(1)} custom-call(s32[16,128]{1,0:T(8,128)} %bitcast.1, f32[3,2048]{1,0:T(4,128)} %points_h.1, f32[3,512]{1,0:T(4,128)} %anchors_h.1, f32[16,2048]{1,0:T(8,128)} %probes_h.1, bf16[1,6,128,128]{3,2,1,0:T(8,128)(2,1)} %tl_h.1, bf16[1,3,128,128]{3,2,1,0:T(8,128)(2,1)} %cl_h.1, bf16[126,128,128]{2,1,0:T(8,128)(2,1)} %tt_h.1, ...), custom_call_target="tpu_custom_call" | custom-call | tf_op jit(solution)/shard_map/hss_product/pallas_call | solution.py:496
  44.4 0.7 %copy.10 = f32[16,2048]{1,0:T(8,128)} copy(f32[16,2048]{1,0:T(8,128)S(1)} %hss_product.1) | data formatting | bytes 262144

commit v7 on v6

--- a/solution.py
+++ b/solution.py
@@ -278,19 +278,23 @@
 
     drows = 128
 
+    half = LEAF // 2
+
     def dense(leaf):
-        @pl.loop(0, LEAF // drows)
-        def _(i):
-            at = pl.ds(pl.multiple_of(leaf * LEAF + i * drows, drows), drows)
-            total = None
-            for c in range(3):
-                left = ptst_v[at, c : c + 1]
-                right = points_v[c : c + 1, leaf * LEAF : (leaf + 1) * LEAF]
-                differ = left - right
-                total = differ * differ if total is None else total + differ * differ
-            hi, lo = split(jnp.exp2((-SHARPNESS * LOG2_E) * total))
-            dhi_v[at, :] = hi
-            dlo_v[at, :] = lo
+        for start, skip in ((0, 0), (half, half)):
+
+            @pl.loop(0, half // drows)
+            def _(i):
+                at = pl.ds(pl.multiple_of(leaf * LEAF + start + i * drows, drows), drows)
+                total = None
+                for c in range(3):
+                    left = ptst_v[at, c : c + 1]
+                    right = points_v[c : c + 1, leaf * LEAF + skip : (leaf + 1) * LEAF]
+                    differ = left - right
+                    total = differ * differ if total is None else total + differ * differ
+                hi, lo = split(jnp.exp2((-SHARPNESS * LOG2_E) * total))
+                dhi_v[at, skip:] = hi
+                dlo_v[at, skip:] = lo
 
     loads[3].wait()
 
@@ -414,7 +418,11 @@
         at = slice(LEAF * i, LEAF * (i + 1))
         hi, lo = split(within[i])
         both = jnp.concatenate([hi, lo], axis=0)
-        inner = fold(dot(x2, dhi_v[at, :])) + dot(x2[:PRB], dlo_v[at, :])
+        upper = slice(LEAF * i, LEAF * i + half)
+        first = fold(dot(x2[:, :half], dhi_v[upper, :half])) + dot(x2[:PRB, :half], dlo_v[upper, :half])
+        first = first + fold(dot_nt(x2[:, half:], dhi_v[upper, half:])) + dot_nt(x2[:PRB, half:], dlo_v[upper, half:])
+        second = fold(dot(x2, dhi_v[at, half:])) + dot(x2[:PRB], dlo_v[at, half:])
+        inner = jnp.concatenate([first, second], axis=1)
         inner = inner + fold(dot_nt(both, bhi_v[at, :])) + dot_nt(hi, blo_v[at, :])
         for b in range(4):
             y_v[4 * i + b] = OUTPUT_SCALE * inner[:, 128 * b : 128 * (b + 1)] + NOISE_VAR * x_v[4 * i + b]

time: 45.1 us -> 45.1 us (level)
  no operation moved by 1% of the time
where the time goes in v7:
time: 45.1 us; the launch traced here: 45 us
  Pallas kernels  44.4 us (98%)
  local copies, waits for them, and re-layouts  0.66 us (1%)
    pallas_call x1, Pallas kernels, body(): pl.pallas_call(kernel, out_shape=pltpu.VMEM((PRB, PTS), F32), in_specs=[p...  44.4 us

profile of v7, /device:TPU:1, one launch (start us, length us, event | category | flops | bytes accessed | tf_op | source)
XLA Modules:
  0.0 45.0 jit_solution(6916705610772023681)
XLA Ops:
  0.0 44.4 %hss_product.1 = f32[16,2048]{1,0:T(8,128)S(1)} custom-call(s32[16,128]{1,0:T(8,128)} %bitcast.1, f32[3,2048]{1,0:T(4,128)} %points_h.1, f32[3,512]{1,0:T(4,128)} %anchors_h.1, f32[16,2048]{1,0:T(8,128)} %probes_h.1, bf16[1,6,128,128]{3,2,1,0:T(8,128)(2,1)} %tl_h.1, bf16[1,3,128,128]{3,2,1,0:T(8,128)(2,1)} %cl_h.1, bf16[126,128,128]{2,1,0:T(8,128)(2,1)} %tt_h.1, ...), custom_call_target="tpu_custom_call" | custom-call | tf_op jit(solution)/shard_map/hss_product/pallas_call | solution.py:504
  44.4 0.7 %copy.10 = f32[16,2048]{1,0:T(8,128)} copy(f32[16,2048]{1,0:T(8,128)S(1)} %hss_product.1) | data formatting | bytes 262144
